TPU v7x, 512 devices: a whole 4x8x8 slice. The times are simulated.
512 devices in a mesh: gx: 64 (over x, y, core), gy: 8 (over z).
Axes of the slice: x: 4, y: 8, z: 8, core: 2. Of those that a mesh axis runs over, the one named last changes fastest.
Arguments:
- cells: int32 [3, 64, 8, 4, 256], P(None, 'gx', 'gy'), may hold values from 1 to 509, as said below
- offsets: float32 [3, 64, 8, 4, 256], P(None, 'gx', 'gy'), may hold values from 0 to 1
- counts: int32 [64, 8, 4], P('gx', 'gy'), may hold values from 16 to 256, as said below
- observed: float32 [64, 8, 4, 256], P('gx', 'gy'), may hold values from -12 to 12
- noise: float32 [64, 8, 4, 256], P('gx', 'gy'), may hold values from 0.1 to 1
- kernel_x: bfloat16 [256, 256], replicated, may hold values from -2 to 2, as said below
- kernel_y: bfloat16 [512, 512], replicated, may hold values from -2 to 2, as said below
- kernel_t: bfloat16 [128, 128], replicated, may hold values from -2 to 2, as said below
Outputs:
- solution: float32 [64, 8, 4, 256], P('gx', 'gy')
- residual: float32 [64, 8, 4, 256], P('gx', 'gy')
Inputs may be any that keep to these rules, and one draw needn't show every extreme that they name: cells[0], cells[1], cells[2] are a slot's x, y and t cell. Slot (bx, by, k, s) has 4 bx <= x < 4 bx + 4 and 64 by + 16 k <= y < 64 by + 16 k + 16; each coordinate lies from 1 to its grid size minus 3. Only the first counts[bx, by, k] slots of tile (bx, by, k) are live; some tile is full. kernel_x is symmetric and positive definite. kernel_y is symmetric and positive definite. kernel_t is symmetric and positive definite.
All inputs are finite; a program needn't handle non-finite values.
Results may differ from a plain program's by a relative error of at most 0.04.
Values may be sent and summed in bfloat16 or wider, within the bound.
A program may use at most 64 MiB of HBM per device.

v0:
```python
import jax
import jax.numpy as jnp
from jax import lax
from jax.sharding import PartitionSpec as P

XS = 4
YS = 64
TY = 16
ITERS = 2


def cubic_weights(fraction):
    square = fraction * fraction
    cubic_term = square * fraction
    return jnp.stack(
        [
            (2.0 * square - cubic_term - fraction) * 0.5,
            (3.0 * cubic_term - 5.0 * square + 2.0) * 0.5,
            (4.0 * square - 3.0 * cubic_term + fraction) * 0.5,
            (cubic_term - square) * 0.5,
        ]
    )


def fold_blocks(pieces, block_axis, below_width, above_width):
    number = pieces.shape[block_axis]
    span_width = pieces.shape[block_axis + 1]
    length = span_width - below_width - above_width
    middle = lax.slice_in_dim(
        pieces, below_width, below_width + length, axis=block_axis + 1
    ).astype(jnp.float32)
    below_rows = lax.slice_in_dim(pieces, 0, below_width, axis=block_axis + 1).astype(jnp.float32)
    above_rows = lax.slice_in_dim(
        pieces, below_width + length, span_width, axis=block_axis + 1
    ).astype(jnp.float32)
    below_zero = jnp.zeros_like(lax.slice_in_dim(below_rows, 0, 1, axis=block_axis))
    above_zero = jnp.zeros_like(lax.slice_in_dim(above_rows, 0, 1, axis=block_axis))
    below_next = jnp.concatenate(
        [lax.slice_in_dim(below_rows, 1, number, axis=block_axis), below_zero], axis=block_axis
    )
    above_prev = jnp.concatenate(
        [above_zero, lax.slice_in_dim(above_rows, 0, number - 1, axis=block_axis)], axis=block_axis
    )
    low_pad = [(0, 0)] * pieces.ndim
    low_pad[block_axis + 1] = (length - below_width, 0)
    high_pad = [(0, 0)] * pieces.ndim
    high_pad[block_axis + 1] = (0, length - above_width)
    summed = middle + jnp.pad(below_next, low_pad) + jnp.pad(above_prev, high_pad)
    new_shape = pieces.shape[:block_axis] + (number * length,) + pieces.shape[block_axis + 2 :]
    return summed.reshape(new_shape)


def widen_blocks(blocks, block_axis, below_width, above_width):
    number = blocks.shape[block_axis]
    length = blocks.shape[block_axis + 1]
    tail_rows = lax.slice_in_dim(blocks, length - below_width, length, axis=block_axis + 1)
    head_rows = lax.slice_in_dim(blocks, 0, above_width, axis=block_axis + 1)
    tail_zero = jnp.zeros_like(lax.slice_in_dim(tail_rows, 0, 1, axis=block_axis))
    head_zero = jnp.zeros_like(lax.slice_in_dim(head_rows, 0, 1, axis=block_axis))
    below_rows = jnp.concatenate(
        [tail_zero, lax.slice_in_dim(tail_rows, 0, number - 1, axis=block_axis)], axis=block_axis
    )
    above_rows = jnp.concatenate(
        [lax.slice_in_dim(head_rows, 1, number, axis=block_axis), head_zero], axis=block_axis
    )
    return jnp.concatenate([below_rows, blocks, above_rows], axis=block_axis + 1)


def dense_weights(local, weights, width):
    columns = lax.broadcasted_iota(jnp.int32, local.shape + (width,), local.ndim)
    total = jnp.zeros(local.shape + (width,), jnp.float32)
    for shift in range(4):
        total = total + weights[shift][..., None] * (
            local[..., None] + shift - 1 == columns
        ).astype(jnp.float32)
    return total


def squared_total(residual):
    return lax.psum(jnp.sum(residual * residual), ("gx", "gy"))


def per_device(cells, offsets, counts, observed, noise, kernel_x, kernel_y, kernel_t):
    groups_x = lax.axis_size("gx")
    groups_y = lax.axis_size("gy")
    block_x = lax.axis_index("gx")
    block_y = lax.axis_index("gy")
    tile_count = counts.shape[2]
    capacity = observed.shape[3]
    grid_y = kernel_y.shape[0]
    time_cells = kernel_t.shape[0]
    time_block = time_cells // groups_y
    y_block = grid_y // groups_x
    wide_x = XS + 3
    wide_y = YS + 3
    tile_wide = TY + 3
    highest = lax.Precision.HIGHEST
    live_mask = (
        lax.broadcasted_iota(jnp.int32, (tile_count, capacity), 1) < counts[0, 0][:, None]
    ).astype(jnp.float32)
    local_cells = cells[:, 0, 0]
    fraction = offsets[:, 0, 0]
    noise_tiles = noise[0, 0]
    tile_start = TY * lax.broadcasted_iota(jnp.int32, (tile_count, capacity), 0)
    local_x = local_cells[0] - XS * block_x + 1
    local_y = local_cells[1] - YS * block_y + 1 - tile_start
    rows_x = dense_weights(local_x, cubic_weights(fraction[0]), wide_x)
    rows_y = dense_weights(local_y, cubic_weights(fraction[1]), tile_wide)
    rows_t = dense_weights(local_cells[2], cubic_weights(fraction[2]), time_cells)
    plane_rows = (rows_x[:, :, :, None] * rows_y[:, :, None, :]).reshape(
        tile_count, capacity, wide_x * tile_wide
    )
    kernel_rows = kernel_y.reshape(groups_x, y_block, grid_y)
    residual = live_mask * observed[0, 0]
    solution = jnp.zeros_like(residual)
    direction = residual
    norm_now = squared_total(residual)
    for iteration in range(ITERS):
        masked = live_mask * direction
        weighted_t = rows_t * masked[:, :, None]
        tile_sums = jnp.einsum(
            "ksp,kst->kpt",
            plane_rows,
            weighted_t,
            precision=highest,
            preferred_element_type=jnp.float32,
        ).reshape(tile_count, wide_x, tile_wide, time_cells)
        slab_sum = jnp.zeros((wide_x, wide_y, time_cells), jnp.float32)
        for tile in range(tile_count):
            slab_sum = slab_sum + jnp.pad(
                tile_sums[tile], ((0, 0), (TY * tile, wide_y - TY * tile - tile_wide), (0, 0))
            )
        spread = jnp.transpose(slab_sum, (0, 2, 1)).astype(jnp.bfloat16)
        timewise = jnp.einsum(
            "st,aty->asy", kernel_t, spread, preferred_element_type=jnp.float32
        ).astype(jnp.bfloat16)
        received = lax.all_to_all(timewise, "gy", split_axis=1, concat_axis=2, tiled=True)
        y_stacked = fold_blocks(
            received.reshape(wide_x, time_block, groups_y, wide_y), 2, 1, 2
        ).astype(jnp.bfloat16)
        y_mixed = jnp.einsum(
            "dkz,atz->adtk", kernel_rows, y_stacked, preferred_element_type=jnp.float32
        ).astype(jnp.bfloat16)
        gathered = lax.all_to_all(
            y_mixed.reshape(wide_x, groups_x, time_block * y_block),
            "gx",
            split_axis=1,
            concat_axis=0,
            tiled=True,
        )
        x_stacked = fold_blocks(
            gathered.reshape(groups_x, wide_x, time_block * y_block), 0, 1, 2
        ).astype(jnp.bfloat16)
        grid_field = jnp.dot(kernel_x, x_stacked, preferred_element_type=jnp.float32).astype(
            jnp.bfloat16
        )
        widened = widen_blocks(grid_field.reshape(groups_x, XS, time_block * y_block), 0, 1, 2)
        returned = lax.all_to_all(
            widened.reshape(groups_x, wide_x, time_block, y_block),
            "gx",
            split_axis=0,
            concat_axis=3,
            tiled=True,
        )
        y_rows = widen_blocks(returned.reshape(wide_x, time_block, groups_y, YS), 2, 1, 2)
        neighbourhood = lax.all_to_all(
            y_rows, "gy", split_axis=2, concat_axis=1, tiled=True
        ).reshape(wide_x, time_cells, wide_y)
        field_rows = jnp.transpose(neighbourhood, (0, 2, 1)).astype(jnp.float32)
        windows = jnp.stack(
            [field_rows[:, TY * tile : TY * tile + tile_wide, :] for tile in range(tile_count)]
        ).reshape(tile_count, wide_x * tile_wide, time_cells)
        picked = jnp.einsum(
            "ksp,kpt->kst",
            plane_rows,
            windows,
            precision=highest,
            preferred_element_type=jnp.float32,
        )
        interpolated = jnp.sum(picked * rows_t, axis=2)
        applied = live_mask * (interpolated + noise_tiles * masked)
        curvature = lax.psum(jnp.sum(direction * applied), ("gx", "gy"))
        step_size = norm_now / curvature
        solution = solution + step_size * direction
        residual = residual - step_size * applied
        if iteration + 1 < ITERS:
            norm_next = squared_total(residual)
            direction = residual + norm_next / norm_now * direction
            norm_now = norm_next
    return (
        solution.reshape(1, 1, tile_count, capacity),
        residual.reshape(1, 1, tile_count, capacity),
    )


def solution(mesh):
    placed = (
        P(None, "gx", "gy", None, None),
        P(None, "gx", "gy", None, None),
        P("gx", "gy", None),
        P("gx", "gy", None, None),
        P("gx", "gy", None, None),
        P(),
        P(),
        P(),
    )
    return jax.shard_map(
        per_device,
        mesh=mesh,
        in_specs=placed,
        out_specs=(P("gx", "gy", None, None), P("gx", "gy", None, None)),
        check_vma=False,
    )
```

profile of v0, /device:TPU:1, one launch (start us, length us, event | category | flops | bytes accessed | tf_op | source)
XLA Modules:
  0.0 455.2 jit_solution(18026898101460209349)
XLA Ops:
  4.0 0.9 fusion.20
  6.0 18.5 %all_to_all.108 = bf16[8,2,3752]{2,1,0:T(2,128)(2,1)S(1)} all-to-all(bf16[8,2,3752]{2,1,0:T(2,128)(2,1)S(1)} %reshape.558), channel_id=1, replica_groups=mesh['gx'=64,'gy'=8] {'gy'}, dimensions={0} | all-to-all | bytes 240128 | tf_op jit(solution)/shard_map/all_to_all | solution.py:137
  26.5 22.5 %all_to_all.109 = bf16[7,64,128]{2,0,1:T(8,128)(2,1)S(1)} all-to-all(bf16[7,64,128]{2,0,1:T(8,128)(2,1)S(1)} %copy.145), channel_id=1, replica_groups=mesh['gx'=64,'gy'=8] {'gx'}, dimensions={1} | all-to-all | bytes 229376 | tf_op jit(solution)/shard_map/all_to_all | solution.py:144
  49.6 1.2 concatenate.82
  51.2 0.9 copy.150
  52.9 1.4 pad_maximum_fusion
  54.3 0.9 copy.152
  55.2 1.0 reshape.560
  56.3 15.0 %all_to_all.110 = bf16[64,2,448]{2,1,0:T(2,128)(2,1)S(1)} all-to-all(bf16[64,2,448]{2,1,0:T(2,128)(2,1)S(1)} %reshape.560), channel_id=1, replica_groups=mesh['gx'=64,'gy'=8] {'gx'}, dimensions={0} | all-to-all | bytes 229376 | tf_op jit(solution)/shard_map/all_to_all | solution.py:158
  73.2 13.7 %all_to_all.111 = bf16[7,16,8,67]{3,1,0,2:T(8,128)(2,1)S(1)} all-to-all(bf16[7,16,8,67]{3,1,0,2:T(8,128)(2,1)S(1)} %copy.154), channel_id=1, replica_groups=mesh['gx'=64,'gy'=8] {'gy'}, dimensions={2} | all-to-all | bytes 240128 | tf_op jit(solution)/shard_map/all_to_all | solution.py:166
  88.4 1.2 fusion.4
  90.4 93.7 %all-reduce.32 = (f32[]{:T(128)}, f32[]{:T(128)}) all-reduce(f32[]{:T(128)} %get-tuple-element.3, f32[]{:T(128)} %get-tuple-element.2), channel_id=1, replica_groups=mesh['gx'=64,'gy'=8] {'gx','gy'}, use_global_device_ids=true, to_apply=%region_1.0 | all-reduce | flops 2 | bytes 16 | tf_op jit(solution)/shard_map/psum | solution.py:80
  186.0 94.9 %psum.30 = f32[]{:T(128)} all-reduce(f32[]{:T(128)} %multiply_reduce_fusion), channel_id=1, replica_groups=mesh['gx'=64,'gy'=8] {'gx','gy'}, use_global_device_ids=true, to_apply=%region_6.7 | all-reduce | flops 1 | bytes 8 | tf_op jit(solution)/shard_map/psum | solution.py:80
  282.3 0.9 fusion.18
  284.2 10.7 %all_to_all.112 = bf16[8,2,3752]{2,1,0:T(2,128)(2,1)S(1)} all-to-all(bf16[8,2,3752]{2,1,0:T(2,128)(2,1)S(1)} %reshape.562), channel_id=1, replica_groups=mesh['gx'=64,'gy'=8] {'gy'}, dimensions={0} | all-to-all | bytes 240128 | tf_op jit(solution)/shard_map/all_to_all | solution.py:137
  297.0 20.1 %all_to_all.113 = bf16[7,64,128]{2,0,1:T(8,128)(2,1)S(1)} all-to-all(bf16[7,64,128]{2,0,1:T(8,128)(2,1)S(1)} %copy.168), channel_id=1, replica_groups=mesh['gx'=64,'gy'=8] {'gx'}, dimensions={1} | all-to-all | bytes 229376 | tf_op jit(solution)/shard_map/all_to_all | solution.py:144
  317.7 1.2 concatenate.95
  319.3 0.9 copy.173
  321.0 1.4 pad_maximum_fusion.1
  323.3 1.0 reshape.564
  324.3 15.0 %all_to_all.114 = bf16[64,2,448]{2,1,0:T(2,128)(2,1)S(1)} all-to-all(bf16[64,2,448]{2,1,0:T(2,128)(2,1)S(1)} %reshape.564), channel_id=1, replica_groups=mesh['gx'=64,'gy'=8] {'gx'}, dimensions={0} | all-to-all | bytes 229376 | tf_op jit(solution)/shard_map/all_to_all | solution.py:158
  341.2 13.9 %all_to_all.115 = bf16[7,16,8,67]{3,1,0,2:T(8,128)(2,1)S(1)} all-to-all(bf16[7,16,8,67]{3,1,0,2:T(8,128)(2,1)S(1)} %copy.177), channel_id=1, replica_groups=mesh['gx'=64,'gy'=8] {'gy'}, dimensions={2} | all-to-all | bytes 240128 | tf_op jit(solution)/shard_map/all_to_all | solution.py:166
  356.8 1.2 fusion.5
  358.7 94.5 %psum.31 = f32[]{:T(128)} all-reduce(f32[]{:T(128)} %fusion.114), channel_id=1, replica_groups=mesh['gx'=64,'gy'=8] {'gx','gy'}, use_global_device_ids=true, to_apply=%region_9.10 | all-reduce | flops 1 | bytes 8 | tf_op jit(solution)/shard_map/psum | solution.py:182
  (176 shorter events, 22.9 us)
Async XLA Ops:
  0.6 48.6 %copy-start = (bf16[256,256]{1,0:T(8,128)(2,1)S(1)}, bf16[256,256]{1,0:T(8,128)(2,1)}, u32[]{:S(2)}) copy-start(bf16[256,256]{1,0:T(8,128)(2,1)} %param.13) | copy-start | bytes 393220
  1.4 1.9 copy-start.19
  2.2 1.1 copy-start.22
  2.2 1.1 copy-start.25
  2.2 1.1 copy-start.28
  3.0 279.2 %copy-start.11 = (f32[4,256]{1,0:T(4,128)}, f32[4,256]{1,0:T(4,128)S(1)}, u32[]{:S(2)}) copy-start(f32[4,256]{1,0:T(4,128)S(1)} %get-tuple-element.36) | copy-start | bytes 12292
  3.0 279.2 %copy-start.13 = (f32[4,256]{1,0:T(4,128)}, f32[4,256]{1,0:T(4,128)S(1)}, u32[]{:S(2)}) copy-start(f32[4,256]{1,0:T(4,128)S(1)} %get-tuple-element.43) | copy-start | bytes 12292
  3.0 279.2 %copy-start.15 = (f32[4,256]{1,0:T(4,128)}, f32[4,256]{1,0:T(4,128)S(1)}, u32[]{:S(2)}) copy-start(f32[4,256]{1,0:T(4,128)S(1)} %get-tuple-element.44) | copy-start | bytes 12292
  3.0 279.2 %copy-start.17 = (f32[4,256]{1,0:T(4,128)}, f32[4,256]{1,0:T(4,128)S(1)}, u32[]{:S(2)}) copy-start(f32[4,256]{1,0:T(4,128)S(1)} %get-tuple-element.46) | copy-start | bytes 12292
  3.2 1.8 copy-start.5
  6.0 19.9 %copy-start.31 = (bf16[512,512]{1,0:T(8,128)(2,1)S(1)}, bf16[512,512]{1,0:T(8,128)(2,1)}, u32[]{:S(2)}) copy-start(bf16[512,512]{1,0:T(8,128)(2,1)} %param.14) | copy-start | bytes 1572868
  87.3 1.1 copy-start.2
  87.4 1.0 copy-start.20
  87.4 1.0 copy-start.23
  88.0 1.6 copy-start.4
  88.0 1.6 copy-start.7
  88.0 1.6 copy-start.8
  89.7 193.9 %copy-start.9 = (f32[4,256]{1,0:T(4,128)}, f32[4,256]{1,0:T(4,128)S(1)}, u32[]{:S(2)}) copy-start(f32[4,256]{1,0:T(4,128)S(1)} %fusion.4) | copy-start | bytes 12292
  89.7 193.6 %copy-start.6 = (bf16[128,128]{1,0:T(8,128)(2,1)S(1)}, bf16[128,128]{1,0:T(8,128)(2,1)}, u32[]{:S(2)}) copy-start(bf16[128,128]{1,0:T(8,128)(2,1)} %param.15) | copy-start | bytes 98308
  284.2 12.1 %copy-start.32 = (bf16[512,512]{1,0:T(8,128)(2,1)S(1)}, bf16[512,512]{1,0:T(8,128)(2,1)}, u32[]{:S(2)}) copy-start(bf16[512,512]{1,0:T(8,128)(2,1)} %param.14) | copy-start | bytes 1572868
  355.7 1.1 copy-start.3
  355.7 1.0 copy-start.12
  355.7 1.0 copy-start.14
  356.4 98.1 %copy-start.10 = (f32[4,256]{1,0:T(4,128)S(1)}, f32[4,256]{1,0:T(4,128)}, u32[]{:S(2)}) copy-start(f32[4,256]{1,0:T(4,128)} %copy-done.9) | copy-start | bytes 12292
  (9 other events, 9.0 us)
where the time goes:
time: 456 us; the launch traced here: 455 us
  blocking collectives  413 us (91%)
  local copies, waits for them, and re-layouts  22.2 us (5%)
  other arithmetic  8.9 us (2%)
  matrix products  6.03 us (1%)
  between operations  5.44 us (1%)
    psum x2, blocking collectives, squared_total(): return lax.psum(jnp.sum(residual * residual), ('gx', 'gy'))  189 us
    psum x1, blocking collectives, per_device(): curvature = lax.psum(jnp.sum(direction * applied), ('gx', 'gy'))  94.5 us
    all_to_all x2, blocking collectives, per_device(): lax.all_to_all(y_mixed.reshape(wide_x, groups_x, time_block * y_block), '...  42.6 us
    all_to_all x2, blocking collectives, per_device(): lax.all_to_all(widened.reshape(groups_x, wide_x, time_block, y_block), 'g...  30.1 us
    all_to_all x2, blocking collectives, per_device(): lax.all_to_all(timewise, 'gy', split_axis=1, concat_axis=2, tiled=True)  29.2 us
    all_to_all x2, blocking collectives, per_device(): lax.all_to_all(y_rows, 'gy', split_axis=2, concat_axis=1, tiled=True)  27.6 us

commit v1 on v0

v1 whole, which is shorter than its diff:
```python
import jax
import jax.numpy as jnp
from jax import lax
from jax.experimental import pallas as pl
from jax.experimental.pallas import tpu as pltpu
from jax.sharding import PartitionSpec as P

XS = 4
YS = 64
ITERS = 2
TILES = 4
CAP = 256
SLOTS = TILES * CAP
CHIPS = 32
GROUP = 16
NX = 256
NY = 512
NT = 128
F32 = jnp.float32
BF16 = jnp.bfloat16
MESH = pl.DeviceIdType.MESH
ROW_ROW = (((1,), (1,)), ((), ()))


def cubic_weights(fraction):
    square = fraction * fraction
    cubic_term = square * fraction
    return (
        (2.0 * square - cubic_term - fraction) * 0.5,
        (3.0 * cubic_term - 5.0 * square + 2.0) * 0.5,
        (4.0 * square - 3.0 * cubic_term + fraction) * 0.5,
        (cubic_term - square) * 0.5,
    )


def iota(shape, axis):
    return lax.broadcasted_iota(jnp.int32, shape, axis)


def flat(rows):
    return jnp.concatenate([rows[k : k + 1, :] for k in range(TILES)], axis=1)


def dot(left, right):
    return jnp.dot(left, right, preferred_element_type=F32)


def dot_rows(left, right):
    return lax.dot_general(left, right, ROW_ROW, preferred_element_type=F32)


def spread_rows(weights, first, rows):
    total = jnp.zeros(rows.shape, F32)
    for shift in range(4):
        total = total + jnp.where(first + shift == rows, weights[shift], 0.0)
    return total


def third(index):
    return (index * 43) >> 7


def kernel(
    cells_ref,
    offsets_ref,
    counts_ref,
    observed_ref,
    noise_ref,
    kx_ref,
    ky_ref,
    kt_ref,
    solution_ref,
    residual_ref,
    plane,
    time_rows,
    mixed_rows,
    mix_y,
    mix_x,
    select,
    turn,
    send_a,
    recv_a,
    send_b,
    recv_b,
    send_c,
    recv_c,
    send_d,
    recv_d,
    sums,
    sums_group,
    sums_chips,
    send_sem,
    recv_sem,
    sum_send_sem,
    sum_recv_sem,
):
    block_x = lax.axis_index("gx")
    block_y = lax.axis_index("gy")
    chip = block_x // 2
    core = block_x % 2
    member = block_y * 2 + core

    def group_device(other):
        return (chip * 2 + other % 2, other // 2)

    def chip_device(other):
        return (other * 2 + core, block_y)

    barrier = pltpu.get_barrier_semaphore()

    def greet_group(step, carry):
        pl.semaphore_signal(
            barrier, inc=1, device_id=group_device((member + step) % GROUP), device_id_type=MESH
        )
        return carry

    def greet_chips(step, carry):
        pl.semaphore_signal(
            barrier, inc=1, device_id=chip_device((chip + step) % CHIPS), device_id_type=MESH
        )
        return carry

    lax.fori_loop(1, GROUP, greet_group, 0)
    lax.fori_loop(1, CHIPS, greet_chips, 0)

    live = jnp.concatenate(
        [(iota((1, CAP), 1) < counts_ref[0, 0, k]).astype(F32) for k in range(TILES)], axis=1
    )
    noise = flat(noise_ref[0, 0])
    start = live * flat(observed_ref[0, 0])
    weights_x = cubic_weights(flat(offsets_ref[0, 0, 0]))
    weights_y = cubic_weights(flat(offsets_ref[1, 0, 0]))
    weights_t = cubic_weights(flat(offsets_ref[2, 0, 0]))
    first_x = flat(cells_ref[0, 0, 0]) - XS * block_x
    first_y = flat(cells_ref[1, 0, 0]) - YS * block_y
    first_t = flat(cells_ref[2, 0, 0]) - 1
    rows_y = spread_rows(weights_y, first_y, iota((YS, SLOTS), 0) + 1)
    for x in range(7):
        row_x = spread_rows(weights_x, first_x, jnp.full((1, SLOTS), x, jnp.int32))
        plane[x * YS : (x + 1) * YS, :] = (row_x * rows_y).astype(BF16)
    edge_row = iota((YS, SLOTS), 0)
    edge_x = third(edge_row)
    edge_y = edge_row - 3 * edge_x
    edge_y = jnp.where(edge_y == 0, 0, YS + edge_y)
    plane[7 * YS :, :] = (
        spread_rows(weights_x, first_x, edge_x) * spread_rows(weights_y, first_y, edge_y)
    ).astype(BF16)
    rows_t = spread_rows(weights_t, first_t, iota((NT, SLOTS), 0)) * live
    time_rows[...] = rows_t
    high = rows_t.astype(BF16)
    low = (rows_t - high.astype(F32)).astype(BF16)
    kt = kt_ref[...]
    mixed_rows[...] = dot(kt, high) + dot(kt, low)

    edge_index = iota((NY, NY), 0)
    slot = edge_index & 63
    slot_x = third(slot)
    slot_y = slot - 3 * slot_x
    cell_y = (edge_index >> 6) * YS + jnp.where(slot_y == 0, -1, YS - 1 + slot_y)
    cell_y = jnp.where(slot < 21, cell_y, -1)
    select[...] = (cell_y == iota((NY, NY), 1)).astype(F32).astype(BF16)
    ky = ky_ref[...]
    mix_y[:NY, :] = ky
    mix_y[NY:, :] = dot(select[...], ky).astype(BF16)
    wide_row = iota((NY, NX), 0)
    wide_x = 2 * (wide_row & 3) + ((wide_row >> 2) & 1)
    cell_x = (wide_row >> 3) * XS - 1 + wide_x
    cell_x = jnp.where(wide_x < 7, cell_x, -1)
    widen = (cell_x == iota((NY, NX), 1)).astype(F32).astype(BF16)
    kx = kx_ref[...]
    mix_x[...] = dot_rows(dot(widen, kx).astype(BF16), widen).astype(BF16)

    def largest_sum(matrix):
        return jnp.max(
            jnp.sum(jnp.abs(matrix.astype(F32)), axis=0, keepdims=True), axis=1, keepdims=True
        )

    scale = 1.0 / (1.0 + largest_sum(kx) * largest_sum(ky) * largest_sum(kt))

    low_half = iota((32, 128), 1) < 64
    edge_lane = third(iota((8, NY), 1) & 63)

    pl.semaphore_wait(barrier, GROUP - 1 + CHIPS - 1)

    def wait_bytes(ref, count, semaphore):
        block = ref.at[pl.ds(0, count)]
        pltpu.make_async_copy(block, block, semaphore).wait()

    def apply_operator(turn_index, vector):
        weighted = (mixed_rows[...] * vector).astype(BF16)
        spread = dot_rows(weighted, plane[...])
        outgoing = jnp.concatenate(
            [
                spread[:, 128 * pair : 128 * (pair + 1)].reshape(GROUP, 8, 128)
                for pair in range(4)
            ],
            axis=1,
        ).astype(BF16)
        send_a[turn_index] = outgoing

        def start_a(step, carry):
            other = (member + step) % GROUP
            pltpu.make_async_remote_copy(
                src_ref=send_a.at[turn_index, other],
                dst_ref=recv_a.at[turn_index, member],
                send_sem=send_sem.at[turn_index, 0],
                recv_sem=recv_sem.at[turn_index, 0],
                device_id=group_device(other),
                device_id_type=MESH,
            ).start()
            return carry

        lax.fori_loop(1, GROUP, start_a, 0)
        recv_a[turn_index, member] = send_a[turn_index, member]
        wait_bytes(recv_a.at[turn_index], GROUP - 1, recv_sem.at[turn_index, 0])

        columns = []
        for pair in range(4):
            evens, odds = [], []
            for half in range(2):
                lower = recv_a[turn_index, 4 * pair + half].astype(F32)
                upper = recv_a[turn_index, 4 * pair + 2 + half].astype(F32)
                even = jnp.where(low_half, lower, pltpu.roll(upper, 64, 1))
                odd = jnp.where(low_half, pltpu.roll(lower, 64, 1), upper)
                evens.append(even)
                odds.append(odd)
            columns.append(jnp.concatenate([evens[0], odds[0], evens[1], odds[1]], axis=0))
        main = jnp.concatenate(columns, axis=1)
        zero = jnp.zeros((8, NY), F32)
        main_parts, edge_parts = [], []
        for half in range(2):
            edge = main[64 * half + 56 : 64 * half + 64, :]
            main_parts.append(main[64 * half : 64 * half + 56, :])
            main_parts.append(zero)
            for row in range(7):
                x = 2 * (row % 4) + row // 4
                edge_parts.append(jnp.where(edge_lane == x, edge, 0.0))
            edge_parts.append(zero)
        left = jnp.concatenate(
            [jnp.concatenate(main_parts, axis=0), jnp.concatenate(edge_parts, axis=0)], axis=1
        ).astype(BF16)
        mixed = dot(left, mix_y[...])

        for row in range(16):
            for quarter in range(4):
                turn[quarter, pl.ds(row, 8, stride=16), :] = mixed[
                    8 * row : 8 * row + 8, 128 * quarter : 128 * (quarter + 1)
                ]
        for quarter in range(4):
            send_b[turn_index, :, quarter] = turn[quarter].reshape(8, 16, 128).astype(BF16)

        def start_b(step, carry):
            other = (chip + step) % CHIPS
            pltpu.make_async_remote_copy(
                src_ref=send_b.at[turn_index, other // 4, other % 4],
                dst_ref=recv_b.at[turn_index, chip],
                send_sem=send_sem.at[turn_index, 1],
                recv_sem=recv_sem.at[turn_index, 1],
                device_id=chip_device(other),
                device_id_type=MESH,
            ).start()
            return carry

        lax.fori_loop(1, CHIPS, start_b, 0)
        recv_b[turn_index, chip] = send_b[turn_index, chip // 4, chip % 4]
        wait_bytes(recv_b.at[turn_index], CHIPS - 1, recv_sem.at[turn_index, 1])

        field = dot(mix_x[...], recv_b[turn_index].reshape(NY, 128))
        send_c[turn_index] = field.astype(BF16).reshape(CHIPS, 16, 128)

        def start_c(step, carry):
            other = (chip + step) % CHIPS
            pltpu.make_async_remote_copy(
                src_ref=send_c.at[turn_index, other],
                dst_ref=recv_c.at[turn_index, chip],
                send_sem=send_sem.at[turn_index, 2],
                recv_sem=recv_sem.at[turn_index, 2],
                device_id=chip_device(other),
                device_id_type=MESH,
            ).start()
            return carry

        lax.fori_loop(1, CHIPS, start_c, 0)
        recv_c[turn_index, chip] = send_c[turn_index, chip]
        wait_bytes(recv_c.at[turn_index], CHIPS - 1, recv_sem.at[turn_index, 2])

        for time in range(8):
            for quarter in range(4):
                turn[quarter, 16 * time : 16 * time + 16, :] = recv_c[
                    turn_index, 4 * time + quarter
                ].astype(F32)
        rows = [
            jnp.concatenate(
                [
                    turn[quarter, pl.ds(row, 8, stride=16), :]
                    for quarter in range(4)
                ],
                axis=1,
            )
            for row in range(16)
        ]
        edges = dot_rows(jnp.concatenate(rows, axis=0).astype(BF16), select[...])
        for half in range(2):
            edge = jnp.zeros((8, NY), F32)
            for row in range(7):
                x = 2 * (row % 4) + row // 4
                first = 64 * half + 8 * row
                edge = edge + jnp.where(edge_lane == x, edges[first : first + 8, :], 0.0)
            even = jnp.concatenate(rows[8 * half : 8 * half + 4], axis=0)
            odd = jnp.concatenate(rows[8 * half + 4 : 8 * half + 7] + [edge], axis=0)
            for pair in range(4):
                lanes = slice(128 * pair, 128 * (pair + 1))
                lower = jnp.where(low_half, even[:, lanes], pltpu.roll(odd[:, lanes], 64, 1))
                upper = jnp.where(low_half, pltpu.roll(even[:, lanes], 64, 1), odd[:, lanes])
                send_d[turn_index, 4 * pair + half] = lower.astype(BF16)
                send_d[turn_index, 4 * pair + 2 + half] = upper.astype(BF16)

        def start_d(step, carry):
            other = (member + step) % GROUP
            pltpu.make_async_remote_copy(
                src_ref=send_d.at[turn_index, other],
                dst_ref=recv_d.at[turn_index, member],
                send_sem=send_sem.at[turn_index, 3],
                recv_sem=recv_sem.at[turn_index, 3],
                device_id=group_device(other),
                device_id_type=MESH,
            ).start()
            return carry

        lax.fori_loop(1, GROUP, start_d, 0)
        recv_d[turn_index, member] = send_d[turn_index, member]
        wait_bytes(recv_d.at[turn_index], GROUP - 1, recv_sem.at[turn_index, 3])

        arrived = recv_d[turn_index].astype(F32)
        around = jnp.concatenate(
            [arrived[:, 8 * pair : 8 * pair + 8, :].reshape(NT, 128) for pair in range(4)], axis=1
        ).astype(BF16)
        picked = dot(around, plane[...])
        interpolated = jnp.sum(picked * time_rows[...], axis=0, keepdims=True)
        return scale * (interpolated + noise * vector)

    once = apply_operator(0, start)
    twice = apply_operator(1, once)

    products = jnp.concatenate(
        [
            start * start,
            start * once,
            once * once,
            start * twice,
            once * twice,
            jnp.zeros((3, SLOTS), F32),
        ],
        axis=0,
    )
    partial = products[:, :128]
    for part in range(1, 8):
        partial = partial + products[:, 128 * part : 128 * (part + 1)]
    sums[0] = partial
    sums_group[member] = partial

    def start_sum_group(step, carry):
        other = (member + step) % GROUP
        pltpu.make_async_remote_copy(
            src_ref=sums.at[0],
            dst_ref=sums_group.at[member],
            send_sem=sum_send_sem.at[0],
            recv_sem=sum_recv_sem.at[0],
            device_id=group_device(other),
            device_id_type=MESH,
        ).start()
        return carry

    lax.fori_loop(1, GROUP, start_sum_group, 0)
    wait_bytes(sums_group, GROUP - 1, sum_recv_sem.at[0])
    partial = jnp.sum(sums_group[...], axis=0)
    sums[1] = partial
    sums_chips[chip] = partial

    def start_sum_chips(step, carry):
        other = (chip + step) % CHIPS
        pltpu.make_async_remote_copy(
            src_ref=sums.at[1],
            dst_ref=sums_chips.at[chip],
            send_sem=sum_send_sem.at[1],
            recv_sem=sum_recv_sem.at[1],
            device_id=chip_device(other),
            device_id_type=MESH,
        ).start()
        return carry

    lax.fori_loop(1, CHIPS, start_sum_chips, 0)
    wait_bytes(sums_chips, CHIPS - 1, sum_recv_sem.at[1])
    totals = jnp.sum(jnp.sum(sums_chips[...], axis=0), axis=1, keepdims=True)
    rr, v0_v1, v1_v1, v0_v2, v1_v2 = [totals[k : k + 1, :] for k in range(5)]
    step_0 = rr / v0_v1
    ratio = step_0 * (v1_v1 / v0_v1)
    new = rr * (ratio - 1.0)
    direction = ratio * start - step_0 * once
    image = ratio * once - step_0 * twice
    curvature = ratio * ratio * v0_v1 - ratio * step_0 * (v1_v1 + v0_v2) + step_0 * step_0 * v1_v2
    step_1 = new / curvature
    solved = scale * (step_0 * start + step_1 * direction)
    rest = start - step_0 * once - step_1 * image
    for k in range(TILES):
        solution_ref[0, 0, k : k + 1, :] = solved[:, CAP * k : CAP * (k + 1)]
        residual_ref[0, 0, k : k + 1, :] = rest[:, CAP * k : CAP * (k + 1)]

    for turn_index in range(ITERS):
        wait_bytes(send_a.at[turn_index], GROUP - 1, send_sem.at[turn_index, 0])
        wait_bytes(recv_b.at[turn_index], CHIPS - 1, send_sem.at[turn_index, 1])
        wait_bytes(send_c.at[turn_index], CHIPS - 1, send_sem.at[turn_index, 2])
        wait_bytes(send_d.at[turn_index], GROUP - 1, send_sem.at[turn_index, 3])
    wait_bytes(sums_group, GROUP - 1, sum_send_sem.at[0])
    wait_bytes(sums_chips, CHIPS - 1, sum_send_sem.at[1])


def per_device(cells, offsets, counts, observed, noise, kernel_x, kernel_y, kernel_t):
    vmem = pl.BlockSpec(memory_space=pltpu.VMEM)
    group_block = (ITERS, GROUP, 32, 128)
    chip_block = (ITERS, CHIPS, 16, 128)
    return pl.pallas_call(
        kernel,
        out_shape=[jax.ShapeDtypeStruct(observed.shape, F32)] * 2,
        in_specs=[vmem, vmem, pl.BlockSpec(memory_space=pltpu.SMEM)] + [vmem] * 5,
        out_specs=[vmem, vmem],
        scratch_shapes=[
            pltpu.VMEM((NY, SLOTS), BF16),
            pltpu.VMEM((NT, SLOTS), F32),
            pltpu.VMEM((NT, SLOTS), F32),
            pltpu.VMEM((2 * NY, NY), BF16),
            pltpu.VMEM((NY, NY), BF16),
            pltpu.VMEM((NY, NY), BF16),
            pltpu.VMEM((4, NT, 128), F32),
            pltpu.VMEM(group_block, BF16),
            pltpu.VMEM(group_block, BF16),
            pltpu.VMEM((ITERS, 8, 4, 16, 128), BF16),
            pltpu.VMEM(chip_block, BF16),
            pltpu.VMEM(chip_block, BF16),
            pltpu.VMEM(chip_block, BF16),
            pltpu.VMEM(group_block, BF16),
            pltpu.VMEM(group_block, BF16),
            pltpu.VMEM((2, 8, 128), F32),
            pltpu.VMEM((GROUP, 8, 128), F32),
            pltpu.VMEM((CHIPS, 8, 128), F32),
            pltpu.SemaphoreType.DMA((ITERS, 4)),
            pltpu.SemaphoreType.DMA((ITERS, 4)),
            pltpu.SemaphoreType.DMA((2,)),
            pltpu.SemaphoreType.DMA((2,)),
        ],
        compiler_params=pltpu.CompilerParams(
            collective_id=0, has_side_effects=True, vmem_limit_bytes=48 * 1024 * 1024
        ),
    )(cells, offsets, counts, observed, noise, kernel_x, kernel_y, kernel_t)


def solution(mesh):
    placed = (
        P(None, "gx", "gy", None, None),
        P(None, "gx", "gy", None, None),
        P("gx", "gy", None),
        P("gx", "gy", None, None),
        P("gx", "gy", None, None),
        P(),
        P(),
        P(),
    )
    return jax.shard_map(
        per_device,
        mesh=mesh,
        in_specs=placed,
        out_specs=(P("gx", "gy", None, None), P("gx", "gy", None, None)),
        check_vma=False,
    )
```

time: 456 us -> 92 us (0.20)
  blocking collectives: 413 us -> 0 us
  Pallas kernels: 0 us -> 83.6 us
  local copies, waits for them, and re-layouts: 22.2 us -> 7.32 us
  other arithmetic: 8.9 us -> 0 us
  matrix products: 6.03 us -> 0 us
  between operations: 5.44 us -> 0.66 us
    psum x3 -> x0, blocking collectives: 283 us -> none  [the longest x2 189 us: squared_total(): return lax.psum(jnp.sum(residual * residual), ('gx', 'gy'))]
    all_to_all x8 -> x0, blocking collectives: 130 us -> none  [the longest x2 42.6 us: per_device(): lax.all_to_all(y_mixed.reshape(wide_x, groups_x, time_block * y_block), '...]
    pallas_call x0 -> x1, Pallas kernels: none -> 83.6 us  [per_device(): pl.pallas_call(kernel, out_shape=[jax.ShapeDtypeStruct(observed.shape, F3...]
    concatenate x14 -> x0, local copies, waits for them, and re-layouts: 8.75 us -> none  [widen_blocks(): jnp.concatenate([below_rows, blocks, above_rows], axis=block_axis + 1)]
    dot_general x10 -> x0, matrix products: 6.03 us -> none  [the longest x2 2.43 us: per_device(): jnp.einsum('ksp,kpt->kst', plane_rows, windows, precision=highest, prefer...]
where the time goes in v1:
time: 92 us; the launch traced here: 91.6 us
  Pallas kernels  83.6 us (91%)
  local copies, waits for them, and re-layouts  7.32 us (8%)
    pallas_call x1, Pallas kernels, per_device(): pl.pallas_call(kernel, out_shape=[jax.ShapeDtypeStruct(observed.shape, F3...  83.6 us
    unnamed x18, local copies, waits for them, and re-layouts  7.32 us

profile of v1, /device:TPU:1, one launch (start us, length us, event | category | flops | bytes accessed | tf_op | source)
XLA Modules:
  0.0 91.6 jit_solution(9484543554764819975)
XLA Ops:
  0.6 0.0 copy-start
  0.6 1.0 %copy-done = bf16[512,512]{1,0:T(8,128)(2,1)S(1)} copy-done((bf16[512,512]{1,0:T(8,128)(2,1)S(1)}, bf16[512,512]{1,0:T(8,128)(2,1)}, u32[]{:S(2)}) %copy-start) | copy-done | bytes 524312
  1.7 0.0 copy-start.1
  1.7 0.9 copy-done.1
  2.6 0.0 copy-start.2
  2.6 0.8 copy-done.2
  3.3 0.0 copy-start.3
  3.3 0.7 copy-done.3
  4.0 0.0 copy-start.4
  4.0 0.7 copy-done.4
  4.8 0.0 copy-start.5
  4.8 0.7 copy-done.5
  5.4 0.0 copy-start.6
  5.4 0.7 copy-done.6
  6.1 0.0 copy-start.7
  6.1 0.7 copy-done.7
  6.8 83.6 %shard_map.95 = (f32[1,1,4,256]{3,2,1,0:T(4,128)S(1)}, f32[1,1,4,256]{3,2,1,0:T(4,128)S(1)}) custom-call(s32[3,1,1,4,256]{4,3,2,1,0:T(4,128)S(1)} %copy-done.3, f32[3,1,1,4,256]{4,3,2,1,0:T(4,128)S(1)} %copy-done.4, s32[1,1,4]{2,1,0:T(1,128)S(1)} %copy-done.7, f32[1,1,4,256]{3,2,1,0:T(4,128)S(1)} %copy-done.5, f32[1,1,4,256]{3,2,1,0:T(4,128)S(1)} %copy-done.6, ...), custom_call_target="tpu_custom_call" | custom-call | tf_op jit(solution)/shard_map/pallas_call | solution.py:422
  90.4 0.6 copy.12
  91.0 0.6 copy.13
Async XLA Ops:
  0.6 1.0 %copy-start = (bf16[512,512]{1,0:T(8,128)(2,1)S(1)}, bf16[512,512]{1,0:T(8,128)(2,1)}, u32[]{:S(2)}) copy-start(bf16[512,512]{1,0:T(8,128)(2,1)} %ky_ref.1) | copy-start | bytes 1572868
  1.7 0.9 copy-start.1
  2.6 0.8 copy-start.2
  3.3 0.7 copy-start.3
  4.0 0.7 copy-start.4
  4.8 0.7 copy-start.5
  5.4 0.7 copy-start.6
  6.1 0.7 copy-start.7

commit v2 on v1

v2 whole, which is shorter than its diff:
```python
import jax
import jax.numpy as jnp
from jax import lax
from jax.experimental import pallas as pl
from jax.experimental.pallas import tpu as pltpu
from jax.sharding import PartitionSpec as P

XS = 4
YS = 64
ITERS = 2
TILES = 4
CAP = 256
SLOTS = TILES * CAP
CHIPS = 32
GROUP = 16
NX = 256
NY = 512
NT = 128
F32 = jnp.float32
BF16 = jnp.bfloat16
MESH = pl.DeviceIdType.MESH
ROW_ROW = (((1,), (1,)), ((), ()))
FAR_X = (2, 1, 3, 0)


def cubic_weights(fraction):
    square = fraction * fraction
    cubic_term = square * fraction
    return (
        (2.0 * square - cubic_term - fraction) * 0.5,
        (3.0 * cubic_term - 5.0 * square + 2.0) * 0.5,
        (4.0 * square - 3.0 * cubic_term + fraction) * 0.5,
        (cubic_term - square) * 0.5,
    )


def iota(shape, axis):
    return lax.broadcasted_iota(jnp.int32, shape, axis)


def flat(rows):
    return jnp.concatenate([rows[k : k + 1, :] for k in range(TILES)], axis=1)


def dot(left, right):
    return jnp.dot(left, right, preferred_element_type=F32)


def dot_rows(left, right):
    return lax.dot_general(left, right, ROW_ROW, preferred_element_type=F32)


def spread_rows(weights, first, rows):
    total = jnp.zeros(rows.shape, F32)
    for shift in range(4):
        total = total + jnp.where(first + shift == rows, weights[shift], 0.0)
    return total


def third(index):
    return (index * 43) >> 7


def lane_sum(row):
    total = row[:, :128]
    for part in range(1, SLOTS // 128):
        total = total + row[:, 128 * part : 128 * (part + 1)]
    return total


def sum_tile(*rows):
    return jnp.concatenate([*rows, jnp.zeros((8 - len(rows), 128), F32)], axis=0)


def totals_of(tile, count):
    totals = jnp.sum(tile, axis=1, keepdims=True)
    return [totals[k : k + 1, :] for k in range(count)]


def kernel(
    cells_hbm,
    offsets_hbm,
    counts_hbm,
    observed_hbm,
    noise_hbm,
    kx_hbm,
    ky_hbm,
    kt_hbm,
    solution_ref,
    residual_ref,
    cells_ref,
    offsets_ref,
    counts_ref,
    observed_ref,
    noise_ref,
    kx_ref,
    ky_ref,
    kt_ref,
    plane,
    time_rows,
    mixed_rows,
    mix_y,
    mix_x,
    select,
    turn,
    send_a,
    recv_a,
    send_b,
    recv_b,
    send_c,
    recv_c,
    send_d,
    recv_d,
    send_ga,
    recv_ga,
    send_gb,
    recv_gb,
    sum_first,
    sum_second,
    sum_group,
    sum_chips,
    load_sem,
    send_sem,
    recv_sem,
    sum_send_sem,
    sum_recv_sem,
):
    block_x = lax.axis_index("gx")
    block_y = lax.axis_index("gy")
    chip = block_x // 2
    core = block_x % 2
    chip_x = chip // 8
    chip_y = chip % 8
    member = block_y * 2 + core

    def far(step):
        return 4 + (step // 2) * (1 - step % 2) - ((step + 1) // 2) * (step % 2)

    def each_of_group(act):
        def one(step, carry):
            z = (block_y + far(step)) % 8
            for other_core in range(2):
                act(z * 2 + other_core, (chip * 2 + other_core, z))
            return carry

        lax.fori_loop(0, 7, one, 0)
        act(block_y * 2 + 1 - core, (chip * 2 + 1 - core, block_y))

    def each_of_chips(act):
        def one(step, carry):
            y = (chip_y + far(step)) % 8
            for shift in FAR_X:
                place = (chip_x + shift) % 4 * 8 + y
                act(place, (place * 2 + core, block_y))
            return carry

        lax.fori_loop(0, 7, one, 0)
        for shift in FAR_X[:3]:
            place = (chip_x + shift) % 4 * 8 + chip_y
            act(place, (place * 2 + core, block_y))

    barrier = pltpu.get_barrier_semaphore()

    def greet(place, device):
        pl.semaphore_signal(barrier, inc=1, device_id=device, device_id_type=MESH)

    loads = [
        pltpu.make_async_copy(source, target, load_sem.at[k])
        for k, (source, target) in enumerate(
            (
                (cells_hbm, cells_ref),
                (offsets_hbm, offsets_ref),
                (counts_hbm, counts_ref),
                (observed_hbm, observed_ref),
                (noise_hbm, noise_ref),
                (kt_hbm, kt_ref),
                (ky_hbm, ky_ref),
                (kx_hbm, kx_ref),
            )
        )
    ]
    for load in loads:
        load.start()
    each_of_chips(greet)
    each_of_group(greet)
    for load in loads[:6]:
        load.wait()

    live = jnp.concatenate(
        [
            (iota((1, CAP), 1) < counts_ref[0, :, k : k + 1]).astype(F32)
            for k in range(TILES)
        ],
        axis=1,
    )
    noise = flat(noise_ref[0, 0])
    start = live * flat(observed_ref[0, 0])
    weights_x = cubic_weights(flat(offsets_ref[0, 0, 0]))
    weights_y = cubic_weights(flat(offsets_ref[1, 0, 0]))
    weights_t = cubic_weights(flat(offsets_ref[2, 0, 0]))
    first_x = flat(cells_ref[0, 0, 0]) - XS * block_x
    first_y = flat(cells_ref[1, 0, 0]) - YS * block_y
    first_t = flat(cells_ref[2, 0, 0]) - 1
    rows_y = spread_rows(weights_y, first_y, iota((YS, SLOTS), 0) + 1)
    for x in range(7):
        row_x = spread_rows(weights_x, first_x, jnp.full((1, SLOTS), x, jnp.int32))
        plane[x * YS : (x + 1) * YS, :] = (row_x * rows_y).astype(BF16)
    edge_row = iota((YS, SLOTS), 0)
    edge_x = third(edge_row)
    edge_y = edge_row - 3 * edge_x
    edge_y = jnp.where(edge_y == 0, 0, YS + edge_y)
    plane[7 * YS :, :] = (
        spread_rows(weights_x, first_x, edge_x) * spread_rows(weights_y, first_y, edge_y)
    ).astype(BF16)
    rows_t = spread_rows(weights_t, first_t, iota((NT, SLOTS), 0)) * live
    time_rows[...] = rows_t
    high = rows_t.astype(BF16)
    low = (rows_t - high.astype(F32)).astype(BF16)
    kt = kt_ref[...]
    mixed_rows[...] = dot(kt, high) + dot(kt, low)

    low_half = iota((32, 128), 1) < 64
    edge_lane = third(iota((8, NY), 1) & 63)

    def wait_bytes(ref, count, semaphore):
        block = ref.at[pl.ds(0, count)]
        pltpu.make_async_copy(block, block, semaphore).wait()

    def copy_group(source, target, sent, received):
        def act(place, device):
            pltpu.make_async_remote_copy(
                src_ref=source(place),
                dst_ref=target.at[member],
                send_sem=sent,
                recv_sem=received,
                device_id=device,
                device_id_type=MESH,
            ).start()

        each_of_group(act)

    def copy_chips(source, target, sent, received):
        def act(place, device):
            pltpu.make_async_remote_copy(
                src_ref=source(place),
                dst_ref=target.at[chip],
                send_sem=sent,
                recv_sem=received,
                device_id=device,
                device_id_type=MESH,
            ).start()

        each_of_chips(act)

    def share_group(which, tile):
        source = sum_second if which != 1 else sum_first
        source[which] = tile
        sum_group[which, member] = tile
        copy_group(
            lambda place: source.at[which],
            sum_group.at[which],
            sum_send_sem.at[which, 0],
            sum_recv_sem.at[which, 0],
        )

    def share_chips(which, tile):
        source = sum_first if which != 1 else sum_second
        source[which] = tile
        sum_chips[which, chip] = tile
        copy_chips(
            lambda place: source.at[which],
            sum_chips.at[which],
            sum_send_sem.at[which, 1],
            sum_recv_sem.at[which, 1],
        )

    def shared_group(which):
        wait_bytes(sum_group.at[which], GROUP - 1, sum_recv_sem.at[which, 0])
        return jnp.sum(sum_group[which], axis=0)

    def shared_chips(which):
        wait_bytes(sum_chips.at[which], CHIPS - 1, sum_recv_sem.at[which, 1])
        return jnp.sum(sum_chips[which], axis=0)

    def time_blocks(spread):
        return jnp.concatenate(
            [
                spread[:, 128 * pair : 128 * (pair + 1)].reshape(GROUP, 8, 128)
                for pair in range(4)
            ],
            axis=1,
        ).astype(BF16)

    def whole_rows(received):
        columns = []
        for pair in range(4):
            parts = []
            for half in range(2):
                lower = received[4 * pair + half].astype(F32)
                upper = received[4 * pair + 2 + half].astype(F32)
                parts.append(jnp.where(low_half, lower, pltpu.roll(upper, 64, 1)))
                parts.append(jnp.where(low_half, pltpu.roll(lower, 64, 1), upper))
            columns.append(jnp.concatenate(parts, axis=0))
        main = jnp.concatenate(columns, axis=1)
        zero = jnp.zeros((8, NY), F32)
        main_parts, edge_parts = [], []
        for half in range(2):
            edge = main[64 * half + 56 : 64 * half + 64, :]
            main_parts.append(main[64 * half : 64 * half + 56, :])
            main_parts.append(zero)
            for row in range(7):
                x = 2 * (row % 4) + row // 4
                edge_parts.append(jnp.where(edge_lane == x, edge, 0.0))
            edge_parts.append(zero)
        return jnp.concatenate(main_parts, axis=0), jnp.concatenate(edge_parts, axis=0)

    def to_column_blocks(rows, target):
        for row in range(16):
            for quarter in range(4):
                turn[quarter, pl.ds(row, 8, stride=16), :] = rows[
                    8 * row : 8 * row + 8, 128 * quarter : 128 * (quarter + 1)
                ]
        for quarter in range(4):
            target[:, quarter] = turn[quarter].reshape(8, 16, 128).astype(BF16)

    def spread_out(turn_index, vector, tile):
        weighted = (mixed_rows[...] * vector).astype(BF16)
        send_a[turn_index] = time_blocks(dot_rows(weighted, plane[...]))
        if turn_index == 0:
            pl.semaphore_wait(barrier, GROUP - 1 + CHIPS - 1)
        copy_group(
            lambda place: send_a.at[turn_index, place],
            recv_a.at[turn_index],
            send_sem.at[turn_index, 0],
            recv_sem.at[turn_index, 0],
        )
        if tile is not None:
            share_group(1, tile)
        recv_a[turn_index, member] = send_a[turn_index, member]
        weighted = (time_rows[...] * vector).astype(BF16)
        send_ga[turn_index] = time_blocks(dot_rows(weighted, plane[...]))
        copy_group(
            lambda place: send_ga.at[turn_index, place],
            recv_ga.at[turn_index],
            send_sem.at[turn_index, 4],
            recv_sem.at[turn_index, 4],
        )
        recv_ga[turn_index, member] = send_ga[turn_index, member]

    def mix_along_y(turn_index):
        wait_bytes(recv_a.at[turn_index], GROUP - 1, recv_sem.at[turn_index, 0])
        main, edge = whole_rows(recv_a[turn_index])
        left = jnp.concatenate([main, edge], axis=1).astype(BF16)
        to_column_blocks(dot(left, mix_y[...]), send_b.at[turn_index])
        copy_chips(
            lambda place: send_b.at[turn_index, place // 4, place % 4],
            recv_b.at[turn_index],
            send_sem.at[turn_index, 1],
            recv_sem.at[turn_index, 1],
        )
        recv_b[turn_index, chip] = send_b[turn_index, chip // 4, chip % 4]
        if turn_index == 1:
            share_chips(1, shared_group(1))
        wait_bytes(recv_ga.at[turn_index], GROUP - 1, recv_sem.at[turn_index, 4])
        main, edge = whole_rows(recv_ga[turn_index])
        to_column_blocks(main + dot(edge.astype(BF16), select[...]), send_gb.at[turn_index])
        copy_chips(
            lambda place: send_gb.at[turn_index, place // 4, place % 4],
            recv_gb.at[turn_index],
            send_sem.at[turn_index, 5],
            recv_sem.at[turn_index, 5],
        )
        recv_gb[turn_index, chip] = send_gb[turn_index, chip // 4, chip % 4]

    def grid_columns(turn_index):
        wait_bytes(recv_b.at[turn_index], CHIPS - 1, recv_sem.at[turn_index, 1])
        return recv_b[turn_index].reshape(NY, 128)

    def spread_columns(turn_index):
        wait_bytes(recv_gb.at[turn_index], CHIPS - 1, recv_sem.at[turn_index, 5])
        return recv_gb[turn_index].reshape(NY, 128).astype(F32)

    def send_field(turn_index, field):
        send_c[turn_index] = field.astype(BF16).reshape(CHIPS, 16, 128)
        copy_chips(
            lambda place: send_c.at[turn_index, place],
            recv_c.at[turn_index],
            send_sem.at[turn_index, 2],
            recv_sem.at[turn_index, 2],
        )
        recv_c[turn_index, chip] = send_c[turn_index, chip]

    def field_back(turn_index, which):
        wait_bytes(recv_c.at[turn_index], CHIPS - 1, recv_sem.at[turn_index, 2])
        for time in range(8):
            for quarter in range(4):
                turn[quarter, 16 * time : 16 * time + 16, :] = recv_c[
                    turn_index, 4 * time + quarter
                ].astype(F32)
        rows = [
            jnp.concatenate(
                [turn[quarter, pl.ds(row, 8, stride=16), :] for quarter in range(4)], axis=1
            )
            for row in range(16)
        ]
        edges = dot_rows(jnp.concatenate(rows, axis=0).astype(BF16), select[...])
        for half in range(2):
            edge = jnp.zeros((8, NY), F32)
            for row in range(7):
                x = 2 * (row % 4) + row // 4
                first = 64 * half + 8 * row
                edge = edge + jnp.where(edge_lane == x, edges[first : first + 8, :], 0.0)
            even = jnp.concatenate(rows[8 * half : 8 * half + 4], axis=0)
            odd = jnp.concatenate(rows[8 * half + 4 : 8 * half + 7] + [edge], axis=0)
            for pair in range(4):
                lanes = slice(128 * pair, 128 * (pair + 1))
                lower = jnp.where(low_half, even[:, lanes], pltpu.roll(odd[:, lanes], 64, 1))
                upper = jnp.where(low_half, pltpu.roll(even[:, lanes], 64, 1), odd[:, lanes])
                send_d[turn_index, 4 * pair + half] = lower.astype(BF16)
                send_d[turn_index, 4 * pair + 2 + half] = upper.astype(BF16)
        copy_group(
            lambda place: send_d.at[turn_index, place],
            recv_d.at[turn_index],
            send_sem.at[turn_index, 3],
            recv_sem.at[turn_index, 3],
        )
        recv_d[turn_index, member] = send_d[turn_index, member]
        share_group(which, shared_chips(which))
        wait_bytes(recv_d.at[turn_index], GROUP - 1, recv_sem.at[turn_index, 3])
        arrived = recv_d[turn_index].astype(F32)
        around = jnp.concatenate(
            [arrived[:, 8 * pair : 8 * pair + 8, :].reshape(NT, 128) for pair in range(4)], axis=1
        ).astype(BF16)
        picked = dot(around, plane[...])
        return jnp.sum(picked * time_rows[...], axis=0, keepdims=True)

    spread_out(0, start, None)

    for load in loads[6:]:
        load.wait()
    edge_index = iota((NY, NY), 0)
    slot = edge_index & 63
    slot_x = third(slot)
    slot_y = slot - 3 * slot_x
    cell_y = (edge_index >> 6) * YS + jnp.where(slot_y == 0, -1, YS - 1 + slot_y)
    cell_y = jnp.where(slot < 21, cell_y, -1)
    select[...] = (cell_y == iota((NY, NY), 1)).astype(F32).astype(BF16)
    ky = ky_ref[...]
    mix_y[:NY, :] = ky
    mix_y[NY:, :] = dot(select[...], ky).astype(BF16)
    wide_row = iota((NY, NX), 0)
    wide_x = 2 * (wide_row & 3) + ((wide_row >> 2) & 1)
    cell_x = (wide_row >> 3) * XS - 1 + wide_x
    cell_x = jnp.where(wide_x < 7, cell_x, -1)
    widen = (cell_x == iota((NY, NX), 1)).astype(F32).astype(BF16)
    mix_x[...] = dot_rows(dot(widen, kx_ref[...]).astype(BF16), widen).astype(BF16)

    mix_along_y(0)
    field = dot(mix_x[...], grid_columns(0))
    send_field(0, field)
    inner = jnp.sum(field * spread_columns(0), axis=0, keepdims=True)
    share_chips(0, sum_tile(lane_sum(start * start), lane_sum(noise * start * start), inner))
    interpolated = field_back(0, 0)
    rr, noise_00, inner = totals_of(shared_group(0), 3)
    step_0 = rr / (inner + noise_00)
    rest = start - step_0 * (interpolated + noise * start)

    spread_out(
        1,
        rest,
        sum_tile(
            lane_sum(rest * rest), lane_sum(noise * rest * rest), lane_sum(noise * rest * start)
        ),
    )
    mix_along_y(1)
    columns = grid_columns(1).astype(F32)
    new, noise_11, noise_01 = totals_of(shared_chips(1), 3)
    ratio = new / rr
    columns = columns + ratio * recv_b[0].reshape(NY, 128).astype(F32)
    field = dot(mix_x[...], columns.astype(BF16))
    send_field(1, field)
    both = spread_columns(1) + ratio * recv_gb[0].reshape(NY, 128).astype(F32)
    share_chips(2, sum_tile(jnp.sum(field * both, axis=0, keepdims=True)))
    interpolated = field_back(1, 2)
    (inner,) = totals_of(shared_group(2), 1)
    curvature = inner + noise_11 + ratio * (2.0 * noise_01 + ratio * noise_00)
    step_1 = new / curvature
    direction = rest + ratio * start
    solved = step_0 * start + step_1 * direction
    rest = rest - step_1 * (interpolated + noise * direction)
    for k in range(TILES):
        solution_ref[0, 0, k : k + 1, :] = solved[:, CAP * k : CAP * (k + 1)]
        residual_ref[0, 0, k : k + 1, :] = rest[:, CAP * k : CAP * (k + 1)]

    for turn_index in range(ITERS):
        wait_bytes(recv_a.at[turn_index], GROUP - 1, send_sem.at[turn_index, 0])
        wait_bytes(recv_b.at[turn_index], CHIPS - 1, send_sem.at[turn_index, 1])
        wait_bytes(recv_c.at[turn_index], CHIPS - 1, send_sem.at[turn_index, 2])
        wait_bytes(recv_d.at[turn_index], GROUP - 1, send_sem.at[turn_index, 3])
        wait_bytes(recv_ga.at[turn_index], GROUP - 1, send_sem.at[turn_index, 4])
        wait_bytes(recv_gb.at[turn_index], CHIPS - 1, send_sem.at[turn_index, 5])
    for which in range(3):
        wait_bytes(sum_group.at[which], GROUP - 1, sum_send_sem.at[which, 0])
        wait_bytes(sum_chips.at[which], CHIPS - 1, sum_send_sem.at[which, 1])


def per_device(cells, offsets, counts, observed, noise, kernel_x, kernel_y, kernel_t):
    vmem = pl.BlockSpec(memory_space=pltpu.VMEM)
    whole = pl.BlockSpec(memory_space=pltpu.HBM)
    group_block = pltpu.VMEM((ITERS, GROUP, 32, 128), BF16)
    chip_block = pltpu.VMEM((ITERS, CHIPS, 16, 128), BF16)
    time_block = pltpu.VMEM((ITERS, 8, 4, 16, 128), BF16)
    operands = (cells, offsets, counts, observed, noise, kernel_x, kernel_y, kernel_t)
    return pl.pallas_call(
        kernel,
        out_shape=[jax.ShapeDtypeStruct(observed.shape, F32)] * 2,
        in_specs=[whole] * 8,
        out_specs=[vmem, vmem],
        scratch_shapes=[pltpu.VMEM(operand.shape, operand.dtype) for operand in operands]
        + [
            pltpu.VMEM((NY, SLOTS), BF16),
            pltpu.VMEM((NT, SLOTS), F32),
            pltpu.VMEM((NT, SLOTS), F32),
            pltpu.VMEM((2 * NY, NY), BF16),
            pltpu.VMEM((NY, NY), BF16),
            pltpu.VMEM((NY, NY), BF16),
            pltpu.VMEM((4, NT, 128), F32),
            group_block,
            group_block,
            time_block,
            chip_block,
            chip_block,
            chip_block,
            group_block,
            group_block,
            group_block,
            group_block,
            time_block,
            chip_block,
            pltpu.VMEM((3, 8, 128), F32),
            pltpu.VMEM((3, 8, 128), F32),
            pltpu.VMEM((3, GROUP, 8, 128), F32),
            pltpu.VMEM((3, CHIPS, 8, 128), F32),
            pltpu.SemaphoreType.DMA((8,)),
            pltpu.SemaphoreType.DMA((ITERS, 6)),
            pltpu.SemaphoreType.DMA((ITERS, 6)),
            pltpu.SemaphoreType.DMA((3, 2)),
            pltpu.SemaphoreType.DMA((3, 2)),
        ],
        compiler_params=pltpu.CompilerParams(
            collective_id=0, has_side_effects=True, vmem_limit_bytes=63 * 1024 * 1024
        ),
    )(*operands)


def solution(mesh):
    placed = (
        P(None, "gx", "gy", None, None),
        P(None, "gx", "gy", None, None),
        P("gx", "gy", None),
        P("gx", "gy", None, None),
        P("gx", "gy", None, None),
        P(),
        P(),
        P(),
    )
    return jax.shard_map(
        per_device,
        mesh=mesh,
        in_specs=placed,
        out_specs=(P("gx", "gy", None, None), P("gx", "gy", None, None)),
        check_vma=False,
    )
```

time: 92 us -> 79.5 us (0.86)
  Pallas kernels: 83.6 us -> 76.8 us
  local copies, waits for them, and re-layouts: 7.32 us -> 1.86 us
    pallas_call x1, Pallas kernels: 83.6 us -> 76.8 us  [per_device(): pl.pallas_call(kernel, out_shape=[jax.ShapeDtypeStruct(observed.shape, F3...]
    unnamed x18 -> x4, local copies, waits for them, and re-layouts: 7.32 us -> 1.86 us
where the time goes in v2:
time: 79.5 us; the launch traced here: 79.3 us
  Pallas kernels  76.8 us (97%)
  local copies, waits for them, and re-layouts  1.86 us (2%)
    pallas_call x1, Pallas kernels, per_device(): pl.pallas_call(kernel, out_shape=[jax.ShapeDtypeStruct(observed.shape, F3...  76.8 us
    unnamed x4, local copies, waits for them, and re-layouts  1.86 us

profile of v2, /device:TPU:1, one launch (start us, length us, event | category | flops | bytes accessed | tf_op | source)
XLA Modules:
  0.0 79.3 jit_solution(13692803678657934545)
XLA Ops:
  0.6 76.8 %shard_map.95 = (f32[1,1,4,256]{3,2,1,0:T(4,128)}, f32[1,1,4,256]{3,2,1,0:T(4,128)}) custom-call(s32[3,1,1,4,256]{4,3,2,1,0:T(4,128)} %cells_hbm.1, f32[3,1,1,4,256]{4,3,2,1,0:T(4,128)} %offsets_hbm.1, s32[1,1,4]{2,1,0:T(1,128)} %counts_hbm.1, f32[1,1,4,256]{3,2,1,0:T(4,128)} %observed_hbm.1, f32[1,1,4,256]{3,2,1,0:T(4,128)} %noise_hbm.1, ...), custom_call_target="tpu_custom_call" | custom-call | tf_op jit(solution)/shard_map/pallas_call | solution.py:514
  77.4 0.0 copy-start
  77.5 1.3 %copy.12 = f32[1,1,4,256]{3,2,1,0:T(4,128)} copy(f32[1,1,4,256]{3,2,1,0:T(4,128)} %get-tuple-element.4) | data formatting | bytes 8192
  78.7 0.0 copy-done
  78.7 0.6 copy.13
Async XLA Ops:
  77.4 1.3 %copy-start = (f32[1,1,4,256]{3,2,1,0:T(4,128)S(1)}, f32[1,1,4,256]{3,2,1,0:T(4,128)}, u32[]{:S(2)}) copy-start(f32[1,1,4,256]{3,2,1,0:T(4,128)} %get-tuple-element.5) | copy-start | bytes 12292

commit v3 on v2

--- a/solution.py
+++ b/solution.py
@@ -21,6 +21,7 @@
 MESH = pl.DeviceIdType.MESH
 ROW_ROW = (((1,), (1,)), ((), ()))
 FAR_X = (2, 1, 3, 0)
+FREE = 88
 
 
 def cubic_weights(fraction):
@@ -68,13 +69,60 @@
     return total
 
 
-def sum_tile(*rows):
-    return jnp.concatenate([*rows, jnp.zeros((8 - len(rows), 128), F32)], axis=0)
-
-
-def totals_of(tile, count):
-    totals = jnp.sum(tile, axis=1, keepdims=True)
-    return [totals[k : k + 1, :] for k in range(count)]
+def sum_row(*rows):
+    lanes = iota((1, 128), 1)
+    total = jnp.zeros((1, 128), F32)
+    for k, row in enumerate(rows):
+        total = jnp.where(lanes == FREE + k, jnp.sum(row, axis=1, keepdims=True), total)
+    return total
+
+
+def totals_of(row, count):
+    return [
+        jnp.sum(jnp.where(iota(row.shape, 1) == FREE + k, row, 0.0), axis=1, keepdims=True)
+        for k in range(count)
+    ]
+
+
+def pieces(row):
+    high = row.astype(BF16).astype(F32)
+    middle = (row - high).astype(BF16).astype(F32)
+    return high, middle, (row - high - middle).astype(BF16).astype(F32)
+
+
+def group_tile(row):
+    rows = iota((8, 128), 0)
+    tile = jnp.zeros((8, 128), F32)
+    for k, piece in enumerate(pieces(row)):
+        tile = jnp.where(rows == k, piece, tile)
+    return tile
+
+
+def chip_tile(row):
+    high, middle, low = pieces(row)
+    rows = iota((16, 128), 0)
+    tile = jnp.where(rows == 7, high + pltpu.roll(low, 8, 1), 0.0)
+    return jnp.where(rows == 15, middle, tile)
+
+
+def group_rows(received):
+    rows = []
+    for member in range(GROUP):
+        tile = received[member, 16:, :].astype(F32)
+        rows.append(tile[8:9, :] + tile[9:10, :] + tile[10:11, :])
+    return jnp.concatenate(rows, axis=0)
+
+
+def chip_rows(received):
+    rows = []
+    for chip in range(CHIPS):
+        tile = received[chip].astype(F32)
+        rows.append(tile[7:8, :] + tile[15:16, :] + pltpu.roll(tile[7:8, :], 120, 1))
+    return jnp.concatenate(rows, axis=0)
+
+
+def quotient(above, below):
+    return jnp.where(below > 0.0, above / jnp.where(below > 0.0, below, 1.0), 0.0)
 
 
 def kernel(
@@ -115,15 +163,14 @@
     recv_ga,
     send_gb,
     recv_gb,
-    sum_first,
-    sum_second,
-    sum_group,
-    sum_chips,
+    sums_sent,
+    sums_chips,
+    sums_group,
     load_sem,
     send_sem,
     recv_sem,
-    sum_send_sem,
-    sum_recv_sem,
+    plain_sem,
+    sum_sem,
 ):
     block_x = lax.axis_index("gx")
     block_y = lax.axis_index("gy")
@@ -252,52 +299,21 @@
 
         each_of_chips(act)
 
-    def share_group(which, tile):
-        source = sum_second if which != 1 else sum_first
-        source[which] = tile
-        sum_group[which, member] = tile
-        copy_group(
-            lambda place: source.at[which],
-            sum_group.at[which],
-            sum_send_sem.at[which, 0],
-            sum_recv_sem.at[which, 0],
-        )
-
-    def share_chips(which, tile):
-        source = sum_first if which != 1 else sum_second
-        source[which] = tile
-        sum_chips[which, chip] = tile
-        copy_chips(
-            lambda place: source.at[which],
-            sum_chips.at[which],
-            sum_send_sem.at[which, 1],
-            sum_recv_sem.at[which, 1],
-        )
-
-    def shared_group(which):
-        wait_bytes(sum_group.at[which], GROUP - 1, sum_recv_sem.at[which, 0])
-        return jnp.sum(sum_group[which], axis=0)
-
-    def shared_chips(which):
-        wait_bytes(sum_chips.at[which], CHIPS - 1, sum_recv_sem.at[which, 1])
-        return jnp.sum(sum_chips[which], axis=0)
-
-    def time_blocks(spread):
-        return jnp.concatenate(
-            [
-                spread[:, 128 * pair : 128 * (pair + 1)].reshape(GROUP, 8, 128)
-                for pair in range(4)
-            ],
-            axis=1,
-        ).astype(BF16)
+    def time_blocks(spread, tile):
+        blocks = [
+            spread[:, 128 * pair : 128 * (pair + 1)].reshape(GROUP, 8, 128) for pair in range(4)
+        ]
+        if tile is not None:
+            blocks[3] = blocks[3] + tile[None]
+        return jnp.concatenate(blocks, axis=1).astype(BF16)
 
     def whole_rows(received):
         columns = []
         for pair in range(4):
             parts = []
             for half in range(2):
-                lower = received[4 * pair + half].astype(F32)
-                upper = received[4 * pair + 2 + half].astype(F32)
+                lower = received[4 * pair + half]
+                upper = received[4 * pair + 2 + half]
                 parts.append(jnp.where(low_half, lower, pltpu.roll(upper, 64, 1)))
                 parts.append(jnp.where(low_half, pltpu.roll(lower, 64, 1), upper))
             columns.append(jnp.concatenate(parts, axis=0))
@@ -314,18 +330,21 @@
             edge_parts.append(zero)
         return jnp.concatenate(main_parts, axis=0), jnp.concatenate(edge_parts, axis=0)
 
-    def to_column_blocks(rows, target):
+    def to_column_blocks(rows, target, tile):
         for row in range(16):
             for quarter in range(4):
                 turn[quarter, pl.ds(row, 8, stride=16), :] = rows[
                     8 * row : 8 * row + 8, 128 * quarter : 128 * (quarter + 1)
                 ]
         for quarter in range(4):
-            target[:, quarter] = turn[quarter].reshape(8, 16, 128).astype(BF16)
+            blocks = turn[quarter].reshape(8, 16, 128)
+            if tile is not None:
+                blocks = blocks + tile[None]
+            target[:, quarter] = blocks.astype(BF16)
 
     def spread_out(turn_index, vector, tile):
         weighted = (mixed_rows[...] * vector).astype(BF16)
-        send_a[turn_index] = time_blocks(dot_rows(weighted, plane[...]))
+        send_a[turn_index] = time_blocks(dot_rows(weighted, plane[...]), tile)
         if turn_index == 0:
             pl.semaphore_wait(barrier, GROUP - 1 + CHIPS - 1)
         copy_group(
@@ -334,24 +353,22 @@
             send_sem.at[turn_index, 0],
             recv_sem.at[turn_index, 0],
         )
-        if tile is not None:
-            share_group(1, tile)
         recv_a[turn_index, member] = send_a[turn_index, member]
+
+    def spread_plain(vector):
         weighted = (time_rows[...] * vector).astype(BF16)
-        send_ga[turn_index] = time_blocks(dot_rows(weighted, plane[...]))
-        copy_group(
-            lambda place: send_ga.at[turn_index, place],
-            recv_ga.at[turn_index],
-            send_sem.at[turn_index, 4],
-            recv_sem.at[turn_index, 4],
-        )
-        recv_ga[turn_index, member] = send_ga[turn_index, member]
-
-    def mix_along_y(turn_index):
+        send_ga[...] = time_blocks(dot_rows(weighted, plane[...]), None)
+        copy_group(lambda place: send_ga.at[place], recv_ga, plain_sem.at[0], plain_sem.at[1])
+        recv_ga[member] = send_ga[member]
+
+    def arrived_blocks(turn_index):
         wait_bytes(recv_a.at[turn_index], GROUP - 1, recv_sem.at[turn_index, 0])
-        main, edge = whole_rows(recv_a[turn_index])
+        return [recv_a[turn_index, place].astype(F32) for place in range(GROUP)]
+
+    def mix_along_y(turn_index, blocks, tile):
+        main, edge = whole_rows(blocks)
         left = jnp.concatenate([main, edge], axis=1).astype(BF16)
-        to_column_blocks(dot(left, mix_y[...]), send_b.at[turn_index])
+        to_column_blocks(dot(left, mix_y[...]), send_b.at[turn_index], tile)
         copy_chips(
             lambda place: send_b.at[turn_index, place // 4, place % 4],
             recv_b.at[turn_index],
@@ -359,26 +376,26 @@
             recv_sem.at[turn_index, 1],
         )
         recv_b[turn_index, chip] = send_b[turn_index, chip // 4, chip % 4]
-        if turn_index == 1:
-            share_chips(1, shared_group(1))
-        wait_bytes(recv_ga.at[turn_index], GROUP - 1, recv_sem.at[turn_index, 4])
-        main, edge = whole_rows(recv_ga[turn_index])
-        to_column_blocks(main + dot(edge.astype(BF16), select[...]), send_gb.at[turn_index])
+
+    def fold_plain():
+        wait_bytes(recv_ga, GROUP - 1, plain_sem.at[1])
+        main, edge = whole_rows([recv_ga[place].astype(F32) for place in range(GROUP)])
+        to_column_blocks(main + dot(edge.astype(BF16), select[...]), send_gb, None)
         copy_chips(
-            lambda place: send_gb.at[turn_index, place // 4, place % 4],
-            recv_gb.at[turn_index],
-            send_sem.at[turn_index, 5],
-            recv_sem.at[turn_index, 5],
+            lambda place: send_gb.at[place // 4, place % 4],
+            recv_gb,
+            plain_sem.at[2],
+            plain_sem.at[3],
         )
-        recv_gb[turn_index, chip] = send_gb[turn_index, chip // 4, chip % 4]
+        recv_gb[chip] = send_gb[chip // 4, chip % 4]
 
     def grid_columns(turn_index):
         wait_bytes(recv_b.at[turn_index], CHIPS - 1, recv_sem.at[turn_index, 1])
         return recv_b[turn_index].reshape(NY, 128)
 
-    def spread_columns(turn_index):
-        wait_bytes(recv_gb.at[turn_index], CHIPS - 1, recv_sem.at[turn_index, 5])
-        return recv_gb[turn_index].reshape(NY, 128).astype(F32)
+    def spread_columns():
+        wait_bytes(recv_gb, CHIPS - 1, plain_sem.at[3])
+        return recv_gb[...].reshape(NY, 128).astype(F32)
 
     def send_field(turn_index, field):
         send_c[turn_index] = field.astype(BF16).reshape(CHIPS, 16, 128)
@@ -390,7 +407,7 @@
         )
         recv_c[turn_index, chip] = send_c[turn_index, chip]
 
-    def field_back(turn_index, which):
+    def field_back(turn_index):
         wait_bytes(recv_c.at[turn_index], CHIPS - 1, recv_sem.at[turn_index, 2])
         for time in range(8):
             for quarter in range(4):
@@ -425,7 +442,8 @@
             recv_sem.at[turn_index, 3],
         )
         recv_d[turn_index, member] = send_d[turn_index, member]
-        share_group(which, shared_chips(which))
+
+    def at_slots(turn_index):
         wait_bytes(recv_d.at[turn_index], GROUP - 1, recv_sem.at[turn_index, 3])
         arrived = recv_d[turn_index].astype(F32)
         around = jnp.concatenate(
@@ -455,39 +473,73 @@
     widen = (cell_x == iota((NY, NX), 1)).astype(F32).astype(BF16)
     mix_x[...] = dot_rows(dot(widen, kx_ref[...]).astype(BF16), widen).astype(BF16)
 
-    mix_along_y(0)
-    field = dot(mix_x[...], grid_columns(0))
-    send_field(0, field)
-    inner = jnp.sum(field * spread_columns(0), axis=0, keepdims=True)
-    share_chips(0, sum_tile(lane_sum(start * start), lane_sum(noise * start * start), inner))
-    interpolated = field_back(0, 0)
-    rr, noise_00, inner = totals_of(shared_group(0), 3)
-    step_0 = rr / (inner + noise_00)
-    rest = start - step_0 * (interpolated + noise * start)
-
-    spread_out(
-        1,
-        rest,
-        sum_tile(
-            lane_sum(rest * rest), lane_sum(noise * rest * rest), lane_sum(noise * rest * start)
-        ),
+    mix_along_y(0, arrived_blocks(0), None)
+    send_field(0, dot(mix_x[...], grid_columns(0)))
+    field_back(0)
+    image_0 = at_slots(0) + noise * start
+
+    sums = sum_row(
+        lane_sum(start * start),
+        lane_sum(start * image_0),
+        lane_sum(image_0 * image_0),
+        lane_sum(noise * start * image_0),
+        lane_sum(noise * image_0 * image_0),
     )
-    mix_along_y(1)
-    columns = grid_columns(1).astype(F32)
-    new, noise_11, noise_01 = totals_of(shared_chips(1), 3)
-    ratio = new / rr
-    columns = columns + ratio * recv_b[0].reshape(NY, 128).astype(F32)
+    own = totals_of(sums, 2)
+    spread_out(1, image_0 - quotient(own[1], own[0]) * start, group_tile(sums))
+    spread_plain(image_0)
+    blocks = arrived_blocks(1)
+    member_sums = group_rows(recv_a[1])
+    group_sums = jnp.sum(member_sums, axis=0, keepdims=True)
+    members = totals_of(member_sums, 2)
+    group = totals_of(group_sums, 2)
+    part = quotient(members[1], members[0]) - quotient(group[1], group[0])
+    blocks = [
+        blocks[place] + part[place : place + 1, :] * recv_a[0, place].astype(F32)
+        for place in range(GROUP)
+    ]
+    mix_along_y(1, blocks, chip_tile(group_sums))
+    fold_plain()
+    grid_columns(1)
+    chip_sums = chip_rows(recv_b[1])
+    chips = totals_of(chip_sums, 2)
+    rr, along, square, noise_01, noise_11 = totals_of(
+        jnp.sum(chip_sums, axis=0, keepdims=True), 5
+    )
+    step_0 = rr / along
+    grow = step_0 * (square / along)
+    ratio = jnp.maximum(grow - 1.0, 0.0)
+    new = rr * ratio
+    part = grow - step_0 * quotient(chips[1], chips[0])
+    columns = jnp.concatenate(
+        [
+            part[place : place + 1, :] * recv_b[0, place].astype(F32)
+            - step_0 * recv_b[1, place].astype(F32)
+            for place in range(CHIPS)
+        ],
+        axis=0,
+    )
     field = dot(mix_x[...], columns.astype(BF16))
     send_field(1, field)
-    both = spread_columns(1) + ratio * recv_gb[0].reshape(NY, 128).astype(F32)
-    share_chips(2, sum_tile(jnp.sum(field * both, axis=0, keepdims=True)))
-    interpolated = field_back(1, 2)
-    (inner,) = totals_of(shared_group(2), 1)
-    curvature = inner + noise_11 + ratio * (2.0 * noise_01 + ratio * noise_00)
+    inner = jnp.sum(jnp.sum(field * spread_columns(), axis=0, keepdims=True), axis=1, keepdims=True)
+    inner = jnp.broadcast_to(inner, (8, 128))
+    sums_sent[0] = inner
+    sums_chips[chip] = inner
+    copy_chips(lambda place: sums_sent.at[0], sums_chips, sum_sem.at[0], sum_sem.at[1])
+    field_back(1)
+    wait_bytes(sums_chips, CHIPS - 1, sum_sem.at[1])
+    inner = jnp.sum(sums_chips[...], axis=0)
+    sums_sent[1] = inner
+    sums_group[member] = inner
+    copy_group(lambda place: sums_sent.at[1], sums_group, sum_sem.at[2], sum_sem.at[3])
+    direction = grow * start - step_0 * image_0
+    image_1 = at_slots(1) + noise * direction
+    wait_bytes(sums_group, GROUP - 1, sum_sem.at[3])
+    inner = jnp.sum(sums_group[...], axis=0)[:1, :1]
+    curvature = -step_0 * (inner + grow * noise_01 - step_0 * noise_11)
     step_1 = new / curvature
-    direction = rest + ratio * start
     solved = step_0 * start + step_1 * direction
-    rest = rest - step_1 * (interpolated + noise * direction)
+    rest = start - step_0 * image_0 - step_1 * image_1
     for k in range(TILES):
         solution_ref[0, 0, k : k + 1, :] = solved[:, CAP * k : CAP * (k + 1)]
         residual_ref[0, 0, k : k + 1, :] = rest[:, CAP * k : CAP * (k + 1)]
@@ -497,11 +549,10 @@
         wait_bytes(recv_b.at[turn_index], CHIPS - 1, send_sem.at[turn_index, 1])
         wait_bytes(recv_c.at[turn_index], CHIPS - 1, send_sem.at[turn_index, 2])
         wait_bytes(recv_d.at[turn_index], GROUP - 1, send_sem.at[turn_index, 3])
-        wait_bytes(recv_ga.at[turn_index], GROUP - 1, send_sem.at[turn_index, 4])
-        wait_bytes(recv_gb.at[turn_index], CHIPS - 1, send_sem.at[turn_index, 5])
-    for which in range(3):
-        wait_bytes(sum_group.at[which], GROUP - 1, sum_send_sem.at[which, 0])
-        wait_bytes(sum_chips.at[which], CHIPS - 1, sum_send_sem.at[which, 1])
+    wait_bytes(recv_ga, GROUP - 1, plain_sem.at[0])
+    wait_bytes(recv_gb, CHIPS - 1, plain_sem.at[2])
+    wait_bytes(sums_chips, CHIPS - 1, sum_sem.at[0])
+    wait_bytes(sums_group, GROUP - 1, sum_sem.at[2])
 
 
 def per_device(cells, offsets, counts, observed, noise, kernel_x, kernel_y, kernel_t):
@@ -533,19 +584,18 @@
             chip_block,
             group_block,
             group_block,
-            group_block,
-            group_block,
-            time_block,
-            chip_block,
-            pltpu.VMEM((3, 8, 128), F32),
-            pltpu.VMEM((3, 8, 128), F32),
-            pltpu.VMEM((3, GROUP, 8, 128), F32),
-            pltpu.VMEM((3, CHIPS, 8, 128), F32),
+            pltpu.VMEM((GROUP, 32, 128), BF16),
+            pltpu.VMEM((GROUP, 32, 128), BF16),
+            pltpu.VMEM((8, 4, 16, 128), BF16),
+            pltpu.VMEM((CHIPS, 16, 128), BF16),
+            pltpu.VMEM((2, 8, 128), F32),
+            pltpu.VMEM((CHIPS, 8, 128), F32),
+            pltpu.VMEM((GROUP, 8, 128), F32),
             pltpu.SemaphoreType.DMA((8,)),
-            pltpu.SemaphoreType.DMA((ITERS, 6)),
-            pltpu.SemaphoreType.DMA((ITERS, 6)),
-            pltpu.SemaphoreType.DMA((3, 2)),
-            pltpu.SemaphoreType.DMA((3, 2)),
+            pltpu.SemaphoreType.DMA((ITERS, 4)),
+            pltpu.SemaphoreType.DMA((ITERS, 4)),
+            pltpu.SemaphoreType.DMA((4,)),
+            pltpu.SemaphoreType.DMA((4,)),
         ],
         compiler_params=pltpu.CompilerParams(
             collective_id=0, has_side_effects=True, vmem_limit_bytes=63 * 1024 * 1024

time: 79.5 us -> 73.4 us (0.923)
  Pallas kernels: 76.8 us -> 70.7 us
    pallas_call x1, Pallas kernels: 76.8 us -> 70.7 us  [per_device(): pl.pallas_call(kernel, out_shape=[jax.ShapeDtypeStruct(observed.shape, F3...]
where the time goes in v3:
time: 73.4 us; the launch traced here: 73.2 us
  Pallas kernels  70.7 us (96%)
  local copies, waits for them, and re-layouts  1.86 us (3%)
    pallas_call x1, Pallas kernels, per_device(): pl.pallas_call(kernel, out_shape=[jax.ShapeDtypeStruct(observed.shape, F3...  70.7 us
    unnamed x4, local copies, waits for them, and re-layouts  1.86 us

profile of v3, /device:TPU:1, one launch (start us, length us, event | category | flops | bytes accessed | tf_op | source)
XLA Modules:
  0.0 73.2 jit_solution(16128322042157850044)
XLA Ops:
  0.6 70.7 %shard_map.95 = (f32[1,1,4,256]{3,2,1,0:T(4,128)}, f32[1,1,4,256]{3,2,1,0:T(4,128)}) custom-call(s32[3,1,1,4,256]{4,3,2,1,0:T(4,128)} %cells_hbm.1, f32[3,1,1,4,256]{4,3,2,1,0:T(4,128)} %offsets_hbm.1, s32[1,1,4]{2,1,0:T(1,128)} %counts_hbm.1, f32[1,1,4,256]{3,2,1,0:T(4,128)} %observed_hbm.1, f32[1,1,4,256]{3,2,1,0:T(4,128)} %noise_hbm.1, ...), custom_call_target="tpu_custom_call" | custom-call | tf_op jit(solution)/shard_map/pallas_call | solution.py:565
  71.3 0.0 copy-start
  71.3 1.3 %copy.12 = f32[1,1,4,256]{3,2,1,0:T(4,128)} copy(f32[1,1,4,256]{3,2,1,0:T(4,128)} %get-tuple-element.4) | data formatting | bytes 8192
  72.6 0.0 copy-done
  72.6 0.6 copy.13
Async XLA Ops:
  71.3 1.3 %copy-start = (f32[1,1,4,256]{3,2,1,0:T(4,128)S(1)}, f32[1,1,4,256]{3,2,1,0:T(4,128)}, u32[]{:S(2)}) copy-start(f32[1,1,4,256]{3,2,1,0:T(4,128)} %get-tuple-element.5) | copy-start | bytes 12292

commit v4 on v3

--- a/solution.py
+++ b/solution.py
@@ -134,8 +134,7 @@
     kx_hbm,
     ky_hbm,
     kt_hbm,
-    solution_ref,
-    residual_ref,
+    result_ref,
     cells_ref,
     offsets_ref,
     counts_ref,
@@ -186,11 +185,16 @@
     def each_of_group(act):
         def one(step, carry):
             z = (block_y + far(step)) % 8
-            for other_core in range(2):
-                act(z * 2 + other_core, (chip * 2 + other_core, z))
+            act(z * 2 + 1 - core, (chip * 2 + 1 - core, z))
             return carry
 
+        def same(step, carry):
+            z = (block_y + far(step)) % 8
+            act(z * 2 + core, (chip * 2 + core, z))
+            return carry
+
         lax.fori_loop(0, 7, one, 0)
+        lax.fori_loop(0, 7, same, 0)
         act(block_y * 2 + 1 - core, (chip * 2 + 1 - core, block_y))
 
     def each_of_chips(act):
@@ -211,6 +215,7 @@
     def greet(place, device):
         pl.semaphore_signal(barrier, inc=1, device_id=device, device_id_type=MESH)
 
+    each_of_chips(greet)
     loads = [
         pltpu.make_async_copy(source, target, load_sem.at[k])
         for k, (source, target) in enumerate(
@@ -228,7 +233,6 @@
     ]
     for load in loads:
         load.start()
-    each_of_chips(greet)
     each_of_group(greet)
     for load in loads[:6]:
         load.wait()
@@ -524,25 +528,25 @@
     inner = jnp.sum(jnp.sum(field * spread_columns(), axis=0, keepdims=True), axis=1, keepdims=True)
     inner = jnp.broadcast_to(inner, (8, 128))
     sums_sent[0] = inner
+    sums_group[member] = inner
+    copy_group(lambda place: sums_sent.at[0], sums_group, sum_sem.at[2], sum_sem.at[3])
+    field_back(1)
+    wait_bytes(sums_group, GROUP - 1, sum_sem.at[3])
+    inner = jnp.sum(sums_group[...], axis=0)
+    sums_sent[1] = inner
     sums_chips[chip] = inner
-    copy_chips(lambda place: sums_sent.at[0], sums_chips, sum_sem.at[0], sum_sem.at[1])
-    field_back(1)
-    wait_bytes(sums_chips, CHIPS - 1, sum_sem.at[1])
-    inner = jnp.sum(sums_chips[...], axis=0)
-    sums_sent[1] = inner
-    sums_group[member] = inner
-    copy_group(lambda place: sums_sent.at[1], sums_group, sum_sem.at[2], sum_sem.at[3])
+    copy_chips(lambda place: sums_sent.at[1], sums_chips, sum_sem.at[0], sum_sem.at[1])
     direction = grow * start - step_0 * image_0
     image_1 = at_slots(1) + noise * direction
-    wait_bytes(sums_group, GROUP - 1, sum_sem.at[3])
-    inner = jnp.sum(sums_group[...], axis=0)[:1, :1]
+    wait_bytes(sums_chips, CHIPS - 1, sum_sem.at[1])
+    inner = jnp.sum(sums_chips[...], axis=0)[:1, :1]
     curvature = -step_0 * (inner + grow * noise_01 - step_0 * noise_11)
     step_1 = new / curvature
     solved = step_0 * start + step_1 * direction
     rest = start - step_0 * image_0 - step_1 * image_1
     for k in range(TILES):
-        solution_ref[0, 0, k : k + 1, :] = solved[:, CAP * k : CAP * (k + 1)]
-        residual_ref[0, 0, k : k + 1, :] = rest[:, CAP * k : CAP * (k + 1)]
+        result_ref[0, 0, 0, k : k + 1, :] = solved[:, CAP * k : CAP * (k + 1)]
+        result_ref[1, 0, 0, k : k + 1, :] = rest[:, CAP * k : CAP * (k + 1)]
 
     for turn_index in range(ITERS):
         wait_bytes(recv_a.at[turn_index], GROUP - 1, send_sem.at[turn_index, 0])
@@ -562,11 +566,11 @@
     chip_block = pltpu.VMEM((ITERS, CHIPS, 16, 128), BF16)
     time_block = pltpu.VMEM((ITERS, 8, 4, 16, 128), BF16)
     operands = (cells, offsets, counts, observed, noise, kernel_x, kernel_y, kernel_t)
-    return pl.pallas_call(
+    result = pl.pallas_call(
         kernel,
-        out_shape=[jax.ShapeDtypeStruct(observed.shape, F32)] * 2,
+        out_shape=jax.ShapeDtypeStruct((2, *observed.shape), F32),
         in_specs=[whole] * 8,
-        out_specs=[vmem, vmem],
+        out_specs=vmem,
         scratch_shapes=[pltpu.VMEM(operand.shape, operand.dtype) for operand in operands]
         + [
             pltpu.VMEM((NY, SLOTS), BF16),
@@ -601,6 +605,7 @@
             collective_id=0, has_side_effects=True, vmem_limit_bytes=63 * 1024 * 1024
         ),
     )(*operands)
+    return result[0], result[1]
 
 
 def solution(mesh):

time: 73.4 us -> 70.5 us (0.960)
  Pallas kernels: 70.7 us -> 68.3 us
    pallas_call x1, Pallas kernels: 70.7 us -> 68.3 us  [per_device(): pl.pallas_call(kernel, out_shape=jax.ShapeDtypeStruct((2, *observed.shape...]
    unnamed x4 -> x0, local copies, waits for them, and re-layouts: 1.86 us -> none
    squeeze x0 -> x1, local copies, waits for them, and re-layouts: none -> 1.28 us  [per_device(): return (result[0], result[1])]
where the time goes in v4:
time: 70.5 us; the launch traced here: 70.3 us
  Pallas kernels  68.3 us (97%)
  local copies, waits for them, and re-layouts  1.28 us (2%)
    pallas_call x1, Pallas kernels, per_device(): pl.pallas_call(kernel, out_shape=jax.ShapeDtypeStruct((2, *observed.shape...  68.3 us

profile of v4, /device:TPU:1, one launch (start us, length us, event | category | flops | bytes accessed | tf_op | source)
XLA Modules:
  0.0 70.3 jit_solution(2127902070288540477)
XLA Ops:
  0.6 68.3 %shard_map.95 = f32[2,1,1,4,256]{4,3,2,1,0:T(4,128)} custom-call(s32[3,1,1,4,256]{4,3,2,1,0:T(4,128)} %cells_hbm.1, f32[3,1,1,4,256]{4,3,2,1,0:T(4,128)} %offsets_hbm.1, s32[1,1,4]{2,1,0:T(1,128)} %counts_hbm.1, f32[1,1,4,256]{3,2,1,0:T(4,128)} %observed_hbm.1, f32[1,1,4,256]{3,2,1,0:T(4,128)} %noise_hbm.1, bf16[256,256]{1,0:T(8,128)(2,1)} %kx_hbm.1, ...), custom_call_target="tpu_custom_call" | custom-call | tf_op jit(solution)/shard_map/pallas_call | solution.py:569
  69.0 1.3 %slice_bitcast_fusion = (f32[1,1,4,256]{3,2,1,0:T(4,128)}, f32[1,1,4,256]{3,2,1,0:T(4,128)}) fusion(f32[2,1,1,4,256]{4,3,2,1,0:T(4,128)} %shard_map.95), kind=kLoop, calls=%fused_computation | loop fusion | bytes 16384 | tf_op jit(solution)/shard_map/squeeze | solution.py:608

commit v5 on v4

--- a/solution.py
+++ b/solution.py
@@ -170,6 +170,7 @@
     recv_sem,
     plain_sem,
     sum_sem,
+    entered,
 ):
     block_x = lax.axis_index("gx")
     block_y = lax.axis_index("gy")
@@ -215,7 +216,31 @@
     def greet(place, device):
         pl.semaphore_signal(barrier, inc=1, device_id=device, device_id_type=MESH)
 
-    each_of_chips(greet)
+    def greet_row(act):
+        for shift in FAR_X[:3]:
+            place = (chip_x + shift) % 4 * 8 + chip_y
+            act(place, (place * 2 + core, block_y))
+
+    def greet_column(act):
+        def one(step, carry):
+            place = chip_x * 8 + (chip_y + far(step)) % 8
+            act(place, (place * 2 + core, block_y))
+            return carry
+
+        lax.fori_loop(0, 7, one, 0)
+
+    def greet_again(place, device):
+        pl.semaphore_signal(entered, inc=1, device_id=device, device_id_type=MESH)
+
+    for step in (4, 3, 5, 2, 6, 1, 7):
+        for other in (0, 1):
+            z = (block_y + step) % 8
+            greet(None, (chip * 2 + other, z))
+    greet(None, (chip * 2 + 1 - core, block_y))
+    for step in (4, 3, 5, 2, 6, 1, 7):
+        place = chip_x * 8 + (chip_y + step) % 8
+        greet(None, (place * 2 + core, block_y))
+    greet_row(greet)
     loads = [
         pltpu.make_async_copy(source, target, load_sem.at[k])
         for k, (source, target) in enumerate(
@@ -233,7 +258,6 @@
     ]
     for load in loads:
         load.start()
-    each_of_group(greet)
     for load in loads[:6]:
         load.wait()
 
@@ -350,13 +374,15 @@
         weighted = (mixed_rows[...] * vector).astype(BF16)
         send_a[turn_index] = time_blocks(dot_rows(weighted, plane[...]), tile)
         if turn_index == 0:
-            pl.semaphore_wait(barrier, GROUP - 1 + CHIPS - 1)
+            pl.semaphore_wait(barrier, GROUP - 1 + 7 + 3)
         copy_group(
             lambda place: send_a.at[turn_index, place],
             recv_a.at[turn_index],
             send_sem.at[turn_index, 0],
             recv_sem.at[turn_index, 0],
         )
+        if turn_index == 0:
+            greet_row(greet_again)
         recv_a[turn_index, member] = send_a[turn_index, member]
 
     def spread_plain(vector):
@@ -373,6 +399,8 @@
         main, edge = whole_rows(blocks)
         left = jnp.concatenate([main, edge], axis=1).astype(BF16)
         to_column_blocks(dot(left, mix_y[...]), send_b.at[turn_index], tile)
+        if turn_index == 0:
+            pl.semaphore_wait(entered, 3)
         copy_chips(
             lambda place: send_b.at[turn_index, place // 4, place % 4],
             recv_b.at[turn_index],
@@ -600,6 +628,7 @@
             pltpu.SemaphoreType.DMA((ITERS, 4)),
             pltpu.SemaphoreType.DMA((4,)),
             pltpu.SemaphoreType.DMA((4,)),
+            pltpu.SemaphoreType.REGULAR,
         ],
         compiler_params=pltpu.CompilerParams(
             collective_id=0, has_side_effects=True, vmem_limit_bytes=63 * 1024 * 1024

time: 70.5 us -> 69.9 us (level)
  no operation moved by 1% of the time
where the time goes in v5:
time: 69.9 us; the launch traced here: 69.7 us
  Pallas kernels  67.8 us (97%)
  local copies, waits for them, and re-layouts  1.28 us (2%)
    pallas_call x1, Pallas kernels, per_device(): pl.pallas_call(kernel, out_shape=jax.ShapeDtypeStruct((2, *observed.shape...  67.8 us

profile of v5, /device:TPU:1, one launch (start us, length us, event | category | flops | bytes accessed | tf_op | source)
XLA Modules:
  0.0 69.7 jit_solution(1036572776399611139)
XLA Ops:
  0.6 67.8 %shard_map.95 = f32[2,1,1,4,256]{4,3,2,1,0:T(4,128)} custom-call(s32[3,1,1,4,256]{4,3,2,1,0:T(4,128)} %cells_hbm.1, f32[3,1,1,4,256]{4,3,2,1,0:T(4,128)} %offsets_hbm.1, s32[1,1,4]{2,1,0:T(1,128)} %counts_hbm.1, f32[1,1,4,256]{3,2,1,0:T(4,128)} %observed_hbm.1, f32[1,1,4,256]{3,2,1,0:T(4,128)} %noise_hbm.1, bf16[256,256]{1,0:T(8,128)(2,1)} %kx_hbm.1, ...), custom_call_target="tpu_custom_call" | custom-call | tf_op jit(solution)/shard_map/pallas_call | solution.py:597
  68.5 1.3 %slice_bitcast_fusion = (f32[1,1,4,256]{3,2,1,0:T(4,128)}, f32[1,1,4,256]{3,2,1,0:T(4,128)}) fusion(f32[2,1,1,4,256]{4,3,2,1,0:T(4,128)} %shard_map.95), kind=kLoop, calls=%fused_computation | loop fusion | bytes 16384 | tf_op jit(solution)/shard_map/squeeze | solution.py:637

commit v6 on v5

--- a/solution.py
+++ b/solution.py
@@ -365,7 +365,7 @@
                     8 * row : 8 * row + 8, 128 * quarter : 128 * (quarter + 1)
                 ]
         for quarter in range(4):
-            blocks = turn[quarter].reshape(8, 16, 128)
+            blocks = turn[quarter, :NT, :].reshape(8, 16, 128)
             if tile is not None:
                 blocks = blocks + tile[None]
             target[:, quarter] = blocks.astype(BF16)
@@ -607,7 +607,7 @@
             pltpu.VMEM((2 * NY, NY), BF16),
             pltpu.VMEM((NY, NY), BF16),
             pltpu.VMEM((NY, NY), BF16),
-            pltpu.VMEM((4, NT, 128), F32),
+            pltpu.VMEM((4, NT + 16, 128), F32),
             group_block,
             group_block,
             time_block,

time: 69.9 us -> 69.9 us (level)
  no operation moved by 1% of the time
where the time goes in v6:
time: 69.9 us; the launch traced here: 69.7 us
  Pallas kernels  67.8 us (97%)
  local copies, waits for them, and re-layouts  1.28 us (2%)
    pallas_call x1, Pallas kernels, per_device(): pl.pallas_call(kernel, out_shape=jax.ShapeDtypeStruct((2, *observed.shape...  67.8 us

profile of v6, /device:TPU:1, one launch (start us, length us, event | category | flops | bytes accessed | tf_op | source)
XLA Modules:
  0.0 69.7 jit_solution(14330217584955316466)
XLA Ops:
  0.6 67.8 %shard_map.95 = f32[2,1,1,4,256]{4,3,2,1,0:T(4,128)} custom-call(s32[3,1,1,4,256]{4,3,2,1,0:T(4,128)} %cells_hbm.1, f32[3,1,1,4,256]{4,3,2,1,0:T(4,128)} %offsets_hbm.1, s32[1,1,4]{2,1,0:T(1,128)} %counts_hbm.1, f32[1,1,4,256]{3,2,1,0:T(4,128)} %observed_hbm.1, f32[1,1,4,256]{3,2,1,0:T(4,128)} %noise_hbm.1, bf16[256,256]{1,0:T(8,128)(2,1)} %kx_hbm.1, ...), custom_call_target="tpu_custom_call" | custom-call | tf_op jit(solution)/shard_map/pallas_call | solution.py:597
  68.5 1.3 %slice_bitcast_fusion = (f32[1,1,4,256]{3,2,1,0:T(4,128)}, f32[1,1,4,256]{3,2,1,0:T(4,128)}) fusion(f32[2,1,1,4,256]{4,3,2,1,0:T(4,128)} %shard_map.95), kind=kLoop, calls=%fused_computation | loop fusion | bytes 16384 | tf_op jit(solution)/shard_map/squeeze | solution.py:637

commit v7 on v6

--- a/solution.py
+++ b/solution.py
@@ -237,10 +237,6 @@
             z = (block_y + step) % 8
             greet(None, (chip * 2 + other, z))
     greet(None, (chip * 2 + 1 - core, block_y))
-    for step in (4, 3, 5, 2, 6, 1, 7):
-        place = chip_x * 8 + (chip_y + step) % 8
-        greet(None, (place * 2 + core, block_y))
-    greet_row(greet)
     loads = [
         pltpu.make_async_copy(source, target, load_sem.at[k])
         for k, (source, target) in enumerate(
@@ -258,6 +254,10 @@
     ]
     for load in loads:
         load.start()
+    for step in (4, 3, 5, 2, 6, 1, 7):
+        place = chip_x * 8 + (chip_y + step) % 8
+        greet(None, (place * 2 + core, block_y))
+    greet_row(greet)
     for load in loads[:6]:
         load.wait()
 

time: 69.9 us -> 70.2 us (level)
  no operation moved by 1% of the time
where the time goes in v7:
time: 70.2 us; the launch traced here: 69.8 us
  Pallas kernels  67.9 us (97%)
  local copies, waits for them, and re-layouts  1.28 us (2%)
    pallas_call x1, Pallas kernels, per_device(): pl.pallas_call(kernel, out_shape=jax.ShapeDtypeStruct((2, *observed.shape...  67.9 us

profile of v7, /device:TPU:1, one launch (start us, length us, event | category | flops | bytes accessed | tf_op | source)
XLA Modules:
  0.0 69.8 jit_solution(8857425263081322591)
XLA Ops:
  0.6 67.9 %shard_map.95 = f32[2,1,1,4,256]{4,3,2,1,0:T(4,128)} custom-call(s32[3,1,1,4,256]{4,3,2,1,0:T(4,128)} %cells_hbm.1, f32[3,1,1,4,256]{4,3,2,1,0:T(4,128)} %offsets_hbm.1, s32[1,1,4]{2,1,0:T(1,128)} %counts_hbm.1, f32[1,1,4,256]{3,2,1,0:T(4,128)} %observed_hbm.1, f32[1,1,4,256]{3,2,1,0:T(4,128)} %noise_hbm.1, bf16[256,256]{1,0:T(8,128)(2,1)} %kx_hbm.1, ...), custom_call_target="tpu_custom_call" | custom-call | tf_op jit(solution)/shard_map/pallas_call | solution.py:597
  68.6 1.3 %slice_bitcast_fusion = (f32[1,1,4,256]{3,2,1,0:T(4,128)}, f32[1,1,4,256]{3,2,1,0:T(4,128)}) fusion(f32[2,1,1,4,256]{4,3,2,1,0:T(4,128)} %shard_map.95), kind=kLoop, calls=%fused_computation | loop fusion | bytes 16384 | tf_op jit(solution)/shard_map/squeeze | solution.py:637
